TPU v7x, 512 devices: a whole 4x4x16 slice. The times are simulated.
512 devices in a mesh: rho: 8 (over y, z_hi), basis: 64 (over x, z_lo, core).
Axes of the slice: x: 4, y: 4, z: 16 (z_hi: 2, z_lo: 8; z = z_hi * 8 + z_lo), core: 2. Of those that a mesh axis runs over, the one named last changes fastest.
Arguments:
- panels: float32 [8, 49152, 256], P('rho', 'basis'), as said below
- end_panels: float32 [2, 49152, 256], P(None, 'basis'), may hold values from -0.02734375 to 0.02734375
- correlation_diag: float32 [49152], P('basis'), may hold values from 2 to 3
- correlation_band: float32 [3, 49152], P(None, 'basis'), may hold values from -0.3 to 0.3
- band_reach: int32 [49152], P('basis'), may hold values from 1 to 3
- sign_rows: int32 [8, 256], P('rho'), may hold values from 0 to 49151
Outputs:
- couplings: float32 [256, 8, 2, 256], P('basis', 'rho')
Inputs may be any that keep to these rules, and one draw needn't show every extreme that they name: panels[k, sign_rows[k, c], c] has magnitude at least 0.5 * 49152 ** -0.5.
All inputs are finite; a program needn't handle non-finite values.
Results may differ from a plain program's by a relative error of at most 0.0003.
Values sent between devices are 32-bit elements; how exact they have to be, the bound alone decides.
No kernel may reach another device: no remote copies, remote signals or barrier semaphores. Data moves between devices by JAX's collectives and lax.ppermute only.
A program may use at most 64 MiB of HBM per device.

v0:
```python
import jax
import jax.numpy as jnp
from jax import lax
from jax.sharding import PartitionSpec as P

radial_step = 0.5


def extended(cells, sides, width):
    for axis, dim in sides:
        count = lax.axis_size(axis)
        ends = count - 1
        head = lax.slice_in_dim(cells, 0, width, axis=dim)
        tail = lax.slice_in_dim(cells, cells.shape[dim] - width, cells.shape[dim], axis=dim)
        cells = jnp.concatenate(
            [
                lax.ppermute(tail, axis, [(i, (i + 1) % count) for i in range(ends)]),
                cells,
                lax.ppermute(head, axis, [((i + 1) % count, i) for i in range(ends)]),
            ],
            axis=dim,
        )
    return cells


def from_behind(array, axis, by):
    count = lax.axis_size(axis)
    pairs = [(i, i + by) for i in range(count) if 0 <= i + by < count]
    return lax.ppermute(array, axis, pairs)


def shards(panels, end_panels, correlation_diag, correlation_band, band_reach, sign_rows):
    r_local, rows, width = panels.shape
    reach = correlation_band.shape[0]
    first_row = lax.axis_index("basis") * rows
    local_rows = sign_rows - first_row
    inside = (local_rows >= 0) & (local_rows < rows)
    clipped = jnp.clip(local_rows, 0, rows - 1)
    picked = jnp.take_along_axis(panels, clipped[:, None, :], axis=1)[:, 0, :]
    probe = lax.psum(jnp.where(inside, picked, jnp.float32(0.0)), "basis")
    fixed = panels * jnp.sign(probe)[:, None, :]
    padded = extended(fixed, (("rho", 0),), 1)
    rho_index = lax.axis_index("rho")
    last_rho = lax.axis_size("rho") - 1
    before_edge = jnp.where(rho_index == 0, end_panels[0], padded[0])
    after_edge = jnp.where(rho_index == last_rho, end_panels[1], padded[-1])
    stacked = jnp.concatenate([before_edge[None], fixed, after_edge[None]], axis=0)
    slope = (stacked[2:] - stacked[:-2]) / (2.0 * radial_step)
    depth = jnp.arange(1, reach + 1)
    band = jnp.where(depth[:, None] <= band_reach[None, :], correlation_band, jnp.float32(0.0))
    band_prior = from_behind(band[:, rows - reach :], "basis", 1)
    band_pad = jnp.concatenate([band_prior, band], axis=1)
    framed = extended(slope, (("basis", 1),), reach)
    applied = correlation_diag[None, :, None] * slope
    for depth_step in range(1, reach + 1):
        upper = framed[:, reach + depth_step : reach + depth_step + rows, :]
        lower = framed[:, reach - depth_step : reach - depth_step + rows, :]
        lower_band = band_pad[depth_step - 1, reach - depth_step : reach - depth_step + rows]
        applied = (
            applied
            + band[depth_step - 1][None, :, None] * upper
            + lower_band[None, :, None] * lower
        )
    left = fixed
    drift = lax.psum_scatter(
        jnp.einsum("ric,rid->crd", left, applied, precision=lax.Precision.HIGHEST),
        "basis",
        scatter_dimension=0,
        tiled=True,
    )
    left = slope
    curve = lax.psum_scatter(
        jnp.einsum("ric,rid->crd", left, applied, precision=lax.Precision.HIGHEST),
        "basis",
        scatter_dimension=0,
        tiled=True,
    )
    result = jnp.stack([drift, curve], axis=2)
    return result


def solution(mesh):
    in_specs = (
        P("rho", "basis", None),
        P(None, "basis", None),
        P("basis"),
        P(None, "basis"),
        P("basis"),
        P("rho", None),
    )
    out_specs = P("basis", "rho", None, None)
    return jax.shard_map(shards, mesh=mesh, in_specs=in_specs, out_specs=out_specs, check_vma=False)
```

profile of v0, /device:TPU:1, one launch (start us, length us, event | category | flops | bytes accessed | tf_op | source)
XLA Modules:
  0.0 1206.2 jit_solution(13178432546275174887)
XLA Ops:
  6.6 0.8 compare_select_fusion.1
  7.5 9.1 gather_fusion
  16.6 0.7 and_select_fusion.1
  17.3 296.6 %psum.7 = f32[1,256]{1,0:T(1,128)S(1)} all-reduce(f32[1,256]{1,0:T(1,128)S(1)} %and_select_fusion.1), channel_id=1, replica_groups=mesh['rho'=8,'basis'=64] {'basis'}, use_global_device_ids=true, to_apply=%region_0.1 | all-reduce | flops 256 | bytes 2048 | tf_op jit(solution)/shard_map/psum | solution.py:40
  313.9 1.3 collective-permute-start
  315.2 13.6 %collective-permute-start.1 = (f32[1,768,256]{2,1,0:T(8,128)S(1)}, f32[1,768,256]{2,1,0:T(8,128)}, u32[]{:S(2)}, u32[]{:S(2)}) collective-permute-start(f32[1,768,256]{2,1,0:T(8,128)S(1)} %broadcast_multiply_fusion), channel_id=1, source_target_pairs={{0,64},{64,128},{128,192},{192,256},{256,320},{320,384},{384,448},... | collective-permute-start | bytes 2359304 | tf_op jit(solution)/shard_map/ppermute | solution.py:17
  328.9 0.1 slice.82
  329.0 4.7 collective-permute-start.3
  333.7 1.6 collective-permute-done
  335.4 1.5 collective-permute-done.1
  336.8 0.2 select_subtract_fusion
  337.1 18.0 %collective-permute-start.2 = (f32[1,3,256]{2,1,0:T(4,128)S(1)}, f32[1,3,256]{2,1,0:T(4,128)S(1)}, u32[]{:S(2)}, u32[]{:S(2)}) collective-permute-start(f32[1,3,256]{2,1,0:T(4,128)S(1)} %get-tuple-element.13), channel_id=1, source_target_pairs={{1,0},{2,1},{3,2},{4,3},{5,4},{6,5},{7,6},{8,7},{9,8},{10,9},{11,1... | collective-permute-start | bytes 9224 | tf_op jit(solution)/shard_map/ppermute | solution.py:19
  355.1 1.9 collective-permute-start.4
  357.0 0.1 maximum_reduce_fusion.1
  357.1 1.0 collective-permute-done.4
  358.1 1.3 fusion.5
  359.4 1.5 convolution_bitcast_fusion.1
  360.9 1.5 convolution_bitcast_fusion
  362.3 0.8 copy.14
  363.2 0.8 copy.15
  364.0 1.3 dynamic-slice
  366.0 832.1 %all-reduce.5.cloned.1.call-done = (f32[256,1,256]{2,1,0:T(1,128)}, f32[256,1,256]{2,1,0:T(1,128)}) async-done(((f32[256,1,256]{2,1,0:T(1,128)}, f32[256,1,256]{2,1,0:T(1,128)}), (f32[256,1,256]{2,1,0:T(1,128)}, f32[256,1,256]{2,1,0:T(1,128)})) %all-reduce.5.cloned.1.call-update) | async-done | bytes 524304
  1198.1 0.7 dynamic-slice_bitcast_fusion
  1198.8 0.6 copy.16
  (23 shorter events, 0.3 us)
Async XLA Ops:
  6.5 307.3 %copy-start = (f32[1,768,256]{2,1,0:T(8,128)S(1)}, f32[1,768,256]{2,1,0:T(8,128)}, u32[]{:S(2)}) copy-start(f32[1,768,256]{2,1,0:T(8,128)} %param.6) | copy-start | bytes 2359300
  6.5 322.3 %copy-start.4 = (s32[768]{0:T(1024)S(1)}, s32[768]{0:T(1024)}, u32[]{:S(2)}) copy-start(s32[768]{0:T(1024)} %param.10) | copy-start | bytes 9220
  6.5 322.3 %copy-start.2 = (f32[3,768]{1,0:T(4,128)S(1)}, f32[3,768]{1,0:T(4,128)}, u32[]{:S(2)}) copy-start(f32[3,768]{1,0:T(4,128)} %param.9) | copy-start | bytes 27652
  6.5 330.3 %copy-start.1 = (f32[2,768,256]{2,1,0:T(8,128)S(1)}, f32[2,768,256]{2,1,0:T(8,128)}, u32[]{:S(2)}) copy-start(f32[2,768,256]{2,1,0:T(8,128)} %param.7) | copy-start | bytes 4718596
  6.5 1191.5 %all-reduce.5.cloned.1.call-start = ((), (), s32[]{:S(2)}) async-start(), calls=%async_computation | async-start | bytes 1048576
  313.9 21.4 %collective-permute-start = (f32[1,768,256]{2,1,0:T(8,128)S(1)}, f32[1,768,256]{2,1,0:T(8,128)S(1)}, u32[]{:S(2)}, u32[]{:S(2)}) collective-permute-start(f32[1,768,256]{2,1,0:T(8,128)S(1)} %broadcast_multiply_fusion), channel_id=1, source_target_pairs={{64,0},{128,64},{192,128},{256,192},{320,256},{384,320},{448,384},... | collective-permute-start | bytes 2359304 | tf_op jit(solution)/shard_map/ppermute | solution.py:19
  315.2 21.6 %collective-permute-start.1 = (f32[1,768,256]{2,1,0:T(8,128)S(1)}, f32[1,768,256]{2,1,0:T(8,128)}, u32[]{:S(2)}, u32[]{:S(2)}) collective-permute-start(f32[1,768,256]{2,1,0:T(8,128)S(1)} %broadcast_multiply_fusion), channel_id=1, source_target_pairs={{0,64},{64,128},{128,192},{192,256},{256,320},{320,384},{384,448},... | collective-permute-start | bytes 2359304 | tf_op jit(solution)/shard_map/ppermute | solution.py:17
  329.0 28.1 %collective-permute-start.3 = (f32[3,3]{1,0:T(4,128)S(1)}, f32[3,3]{1,0:T(4,128)S(1)}, u32[]{:S(2)}, u32[]{:S(2)}) collective-permute-start(f32[3,3]{1,0:T(4,128)S(1)} %slice.82), channel_id=1, source_target_pairs={{0,1},{1,2},{2,3},{3,4},{4,5},{5,6},{6,7},{7,8},{8,9},{9,10},{10,1... | collective-permute-start | bytes 116 | tf_op jit(solution)/shard_map/ppermute | solution.py:29
  333.7 24.4 %copy-start.3 = (f32[768]{0:T(1024)S(1)}, f32[768]{0:T(1024)}, u32[]{:S(2)}) copy-start(f32[768]{0:T(1024)} %param.8) | copy-start | bytes 9220
  337.1 20.1 %collective-permute-start.2 = (f32[1,3,256]{2,1,0:T(4,128)S(1)}, f32[1,3,256]{2,1,0:T(4,128)S(1)}, u32[]{:S(2)}, u32[]{:S(2)}) collective-permute-start(f32[1,3,256]{2,1,0:T(4,128)S(1)} %get-tuple-element.13), channel_id=1, source_target_pairs={{1,0},{2,1},{3,2},{4,3},{5,4},{6,5},{7,6},{8,7},{9,8},{10,9},{11,1... | collective-permute-start | bytes 9224 | tf_op jit(solution)/shard_map/ppermute | solution.py:19
  355.1 3.1 collective-permute-start.4
Sparse Core Ops, SparseCore 0:
  364.2 833.8 all-reduce.4
where the time goes:
time: 1210 us
  waiting for transfers between devices  836 us (69%)
  blocking collectives  297 us (25%)
  starting transfers between devices  39.6 us (3%)
  between operations  14.2 us (1%)
  local copies, waits for them, and re-layouts  13.5 us (1%)
    unnamed x2, waiting for transfers between devices  832 us
    psum x1, blocking collectives, shards(): probe = lax.psum(jnp.where(inside, picked, jnp.float32(0.0)), 'basis')  297 us
  transfers between devices with their start and end apart: 6, of which 4 were waited for; matrix products, arithmetic and copies ran while one was open for 0% of the time, Pallas kernels for 0%

commit v1 on v0

v1 whole, which is shorter than its diff:
```python
import jax
import jax.numpy as jnp
from jax import lax
from jax.sharding import PartitionSpec as P

radial_step = 0.5
edge = 8
both = ("rho", "basis")
exact = lax.Precision.HIGHEST


def hops(target):
    pairs = []
    for rho in range(8):
        for basis in range(64):
            to = target(rho // 2, rho % 2, basis // 16, basis // 2 % 8, basis % 2)
            if to is not None:
                y, h, x, z, core = to
                pairs.append((rho * 64 + basis, (y * 2 + h) * 64 + x * 16 + z * 2 + core))
    return pairs


def basis_step(x, z, core, by):
    index = (x * 16 + z * 2 + core + by) % 64
    return index // 16, index // 2 % 8, index % 2


def move(array, target):
    return lax.ppermute(array, both, hops(target))


x_groups = [[x * 16 + rest for x in range(4)] for rest in range(16)]
z_groups = [[x * 16 + z * 2 + core for z in range(8)] for x in range(4) for core in range(2)]


def spread(array, groups):
    return lax.all_to_all(array, "basis", 0, 0, axis_index_groups=groups)


def gather_sum(vector, groups):
    count = len(groups[0])
    return spread(jnp.broadcast_to(vector[None], (count, *vector.shape)), groups).sum(0)


def swap_core(y, h, x, z, core):
    return y, h, x, z, 1 - core


def swap_parity(y, h, x, z, core):
    return y, 1 - h, x, z, core


def to_neighbour(y, h, x, z, core):
    to = y - 1 if h == 0 else y + 1
    return (to, h, x, z, core) if 0 <= to < 4 else None


def from_neighbour(y, h, x, z, core):
    to = y + 1 if h == 0 else y - 1
    return (to, h, x, z, core) if 0 <= to < 4 else None


def halo_own(y, h, x, z, core):
    return (y, h, *basis_step(x, z, core, 1 if h == 0 else -1))


def halo_visitor(y, h, x, z, core):
    return (y, 1 - h, *basis_step(x, z, core, -1 if h == 0 else 1))


def halo_neighbour(y, h, x, z, core):
    to = (y - 1) % 4 if h == 0 else (y + 1) % 4
    return (to, h, *basis_step(x, z, core, 1 if h == 0 else -1))


def banded(field, diag, band):
    reach, rows = band.shape
    total = diag[:, None] * field
    for d in range(1, reach + 1):
        weight = band[d - 1, : rows - d, None]
        total = total + jnp.pad(weight * field[d:], ((0, d), (0, 0)))
        total = total + jnp.pad(weight * field[: rows - d], ((d, 0), (0, 0)))
    return total


def product(a, b):
    return lax.dot_general(a, b, (((0,), (0,)), ((), ())), precision=exact)


def shards(panels, end_panels, correlation_diag, correlation_band, band_reach, sign_rows):
    own = panels[0]
    rows, width = own.shape
    reach = correlation_band.shape[0]
    half = rows // 2
    rho, basis = lax.axis_index("rho"), lax.axis_index("basis")
    y, h, core = rho // 2, rho % 2, basis % 2
    even = h == 0

    visitor = move(lax.dynamic_slice_in_dim(own, (1 - h) * (half - edge), half + edge), swap_parity)
    near = move(own, to_neighbour)

    local_rows = sign_rows[0] - basis * rows
    hit = lax.broadcasted_iota(jnp.int32, (rows, width), 0) == local_rows[None, :]
    picked = jnp.where(hit, own, 0.0).sum(0)
    depth = jnp.arange(1, reach + 1)[:, None]
    band = jnp.where(depth <= band_reach[None, :], correlation_band, 0.0)

    end_far = jnp.where(even, end_panels[1], end_panels[0])
    end_near = jnp.where(even, end_panels[0], end_panels[1])
    at_far = jnp.where(even, y == 3, y == 0)
    at_near = jnp.where(even, y == 0, y == 3)

    def rim(array):
        return jnp.where(even, array[rows - edge :], array[:edge])

    tail = jnp.pad(band[:, rows - edge :], ((0, edge - reach), (0, width - edge)))
    own_rim = move(jnp.concatenate([rim(own), tail]), halo_own)
    near_rim = move(
        jnp.concatenate(
            [jnp.where(at_near, rim(end_far), rim(own)), jnp.broadcast_to(picked[None], (edge, width))]
        ),
        halo_neighbour,
    )
    visitor_rim = move(
        jnp.concatenate(
            [own[rows - edge :], end_panels[0, rows - edge :], jnp.broadcast_to(picked[None], (edge, width))]
        ),
        halo_visitor,
    )
    probe = jnp.stack([picked, near_rim[edge], visitor_rim[2 * edge]] + [jnp.zeros_like(picked)] * 5)
    probe = probe + move(probe, swap_core)
    probe = gather_sum(probe, x_groups)
    probe = gather_sum(probe, z_groups)
    signs = jnp.sign(probe)
    own_sign, visitor_sign = signs[0], signs[2]
    near_sign = jnp.where(at_far, 1.0, signs[1])

    has_low = even & (basis > 0)
    has_high = (h == 1) & (basis < 63)

    def framed(array, halo):
        return jnp.concatenate([jnp.where(has_low, halo, 0.0), array, jnp.where(has_high, halo, 0.0)])

    own_frame = framed(own, own_rim[:edge]) * own_sign
    near_frame = framed(jnp.where(at_far, end_far, near), near_rim[:edge]) * near_sign
    slope = jnp.where(even, near_frame - own_frame, own_frame - near_frame) / (2.0 * radial_step)
    before = own_rim[edge : edge + reach, :edge]
    inward = jnp.arange(edge)[None, :] + depth >= edge
    band_frame = jnp.concatenate(
        [jnp.where(has_low & inward, before, 0.0), band, jnp.zeros((reach, edge), jnp.float32)], axis=1
    )
    diag_frame = jnp.pad(correlation_diag, (edge, edge))
    applied = banded(slope, diag_frame, band_frame)
    curve = product(slope, applied)

    def window(array, axis=0):
        return lax.dynamic_slice_in_dim(array, h * half, half + 2 * edge, axis)

    place = jnp.arange(half + 2 * edge)[:, None]
    inner = (place >= edge) & (place < edge + half)
    diag_window, band_window = window(diag_frame), window(band_frame, 1)

    def crossed(array):
        source = jnp.where(inner | (h == 1), window(array), 0.0)
        return jnp.where(inner | even, banded(source, diag_window, band_window), 0.0)

    own_applied, near_applied, slope_applied = crossed(own_frame), crossed(near_frame), crossed(slope)

    blank = jnp.zeros((edge, width), jnp.float32)
    seen = jnp.where(
        even, jnp.concatenate([visitor_rim[:edge], visitor]), jnp.concatenate([visitor, blank])
    ) * visitor_sign
    end_frame = jnp.concatenate([visitor_rim[edge : 2 * edge], end_near, blank])
    beside = jnp.where(at_near, window(end_frame), 0.0)
    cross = product(seen, slope_applied)
    first = product(own_applied, (seen - beside) / (2.0 * radial_step))
    second = product(near_applied, seen / (2.0 * radial_step))

    parts = jnp.stack([cross, curve, first, second])
    parts = parts.reshape(4, 4, 8, 2, 4, width).transpose(3, 1, 2, 0, 4, 5).reshape(2, 4, 8, 16, width)
    mine = lax.dynamic_index_in_dim(parts, core, 0, keepdims=False)
    other = lax.dynamic_index_in_dim(parts, 1 - core, 0, keepdims=False)
    mine = mine + move(other, swap_core)
    mine = spread(mine, x_groups).sum(0)
    mine = spread(mine, z_groups).sum(0)
    away, home = mine[:8], mine[8:]
    away = move(away, swap_parity)
    second = move(home, from_neighbour)[4:]
    turn = jnp.where(even, 1.0, -1.0)
    drift = turn * (home[:4] - second) + away[:4]
    curve = away[4:]
    return jnp.stack([drift, curve], axis=1)[:, None]


def solution(mesh):
    in_specs = (
        P("rho", "basis", None),
        P(None, "basis", None),
        P("basis"),
        P(None, "basis"),
        P("basis"),
        P("rho", None),
    )
    out_specs = P("basis", "rho", None, None)
    return jax.shard_map(shards, mesh=mesh, in_specs=in_specs, out_specs=out_specs, check_vma=False)
```

time: 1210 us -> 168 us (0.14)
  the two profiles are of different devices: /device:TPU:1 before, /device:TPU:8 now
where the time goes in v1:
time: 168 us; the launch traced here: 167 us
  starting transfers between devices  73.7 us (44%)
  blocking collectives  26.4 us (16%)
  waiting for transfers between devices  25.1 us (15%)
  local copies, waits for them, and re-layouts  17.3 us (10%)
  other arithmetic  14.7 us (9%)
  matrix products  9.59 us (6%)
    ppermute x9, starting transfers between devices, move(): return lax.ppermute(array, both, hops(target))  46 us
    all_to_all x2, starting transfers between devices, spread(): return lax.all_to_all(array, 'basis', 0, 0, axis_index_groups=groups)  27.7 us
    all_to_all x2, blocking collectives, spread(): return lax.all_to_all(array, 'basis', 0, 0, axis_index_groups=groups)  26.4 us
    all_to_all x2, waiting for transfers between devices, spread(): return lax.all_to_all(array, 'basis', 0, 0, axis_index_groups=groups)  13.7 us
    ppermute x9, waiting for transfers between devices, move(): return lax.ppermute(array, both, hops(target))  11.3 us
    dot_general x4, matrix products, product(): return lax.dot_general(a, b, (((0,), (0,)), ((), ())), precision=exact)  9.59 us
    mul x6, other arithmetic, banded(): total = total + jnp.pad(weight * field[d:], ((0, d), (0, 0)))  4.66 us
    slice x6, local copies, waits for them, and re-layouts, banded(): weight = band[d - 1, :rows - d, None]  3.81 us
  transfers between devices with their start and end apart: 11, of which 5 were waited for; matrix products, arithmetic and copies ran while one was open for 16% of the time, Pallas kernels for 0%

profile of v1, /device:TPU:8, one launch (start us, length us, event | category | flops | bytes accessed | tf_op | source)
XLA Modules:
  0.0 167.4 jit_solution(4675208470825023755)
XLA Ops:
  0.0 7.9 %collective-permute-start.4 = (f32[768,256]{1,0:T(8,128)}, f32[768,256]{1,0:T(8,128)}, u32[]{:S(2)}, u32[]{:S(2)}) collective-permute-start(f32[768,256]{1,0:T(8,128)} %bitcast.42), channel_id=1, source_target_pairs={{64,192},{65,193},{66,194},{67,195},{68,196},{69,197},{70,198},{71... | collective-permute-start | bytes 2359304 | tf_op jit(solution)/shard_map/ppermute | solution.py:29
  11.9 8.5 %collective-permute-start = (f32[24,256]{1,0:T(8,128)}, f32[24,256]{1,0:T(8,128)}, u32[]{:S(2)}, u32[]{:S(2)}) collective-permute-start(f32[24,256]{1,0:T(8,128)} %pad_maximum_fusion.1), channel_id=1, source_target_pairs={{0,127},{1,64},{2,65},{3,66},{4,67},{5,68},{6,69},{7,70},{8,71},{9... | collective-permute-start | bytes 73736 | tf_op jit(solution)/shard_map/ppermute | solution.py:29
  20.4 1.8 %dynamic-slice_bitcast_fusion.1 = f32[392,256]{1,0:T(8,128)} fusion(f32[1,768,256]{2,1,0:T(8,128)} %param.6, s32[]{:T(128)S(6)} %select_n.183), kind=kLoop, calls=%fused_computation.107 | loop fusion | bytes 802820 | tf_op jit(solution)/shard_map/dynamic_slice | solution.py:99
  22.2 4.9 %collective-permute-start.1 = (f32[392,256]{1,0:T(8,128)}, f32[392,256]{1,0:T(8,128)S(1)}, u32[]{:S(2)}, u32[]{:S(2)}) collective-permute-start(f32[392,256]{1,0:T(8,128)} %dynamic-slice_bitcast_fusion.1), channel_id=1, source_target_pairs={{0,64},{1,65},{2,66},{3,67},{4,68},{5,69},{6,70},{7,71},{8,72},{9,... | collective-permute-start | bytes 1204232 | tf_op jit(solution)/shard_map/ppermute | solution.py:29
  30.5 2.4 %bitcast_select_fusion = (f32[768,256]{1,0:T(8,128)}, f32[1,768,256]{2,1,0:T(8,128)S(1)}) fusion(f32[768,256]{1,0:T(8,128)} %collective-permute-done.4, pred[]{:T(512)S(6)} %select_n.200, f32[2,768,256]{2,1,0:T(8,128)S(1)} %copy-done, pred[]{:T(512)S(6)} %eq.30), kind=kLoop, calls=%fused_computation.27 | loop fusion | flops 393216 | bytes 3932162 | tf_op jit(solution)/shard_map/jit(_where)/select_n | solution.py:145
  32.9 3.0 %collective-permute-start.2 = (f32[16,256]{1,0:T(8,128)S(1)}, f32[16,256]{1,0:T(8,128)S(1)}, u32[]{:S(2)}, u32[]{:S(2)}) collective-permute-start(f32[16,256]{1,0:T(8,128)S(1)} %pad_maximum_fusion.2), channel_id=1, source_target_pairs={{0,385},{1,386},{2,387},{3,388},{4,389},{5,390},{6,391},{7,392},{8... | collective-permute-start | bytes 49160 | tf_op jit(solution)/shard_map/ppermute | solution.py:29
  35.9 2.8 %collective-permute-start.5 = (f32[16,256]{1,0:T(8,128)S(1)}, f32[16,256]{1,0:T(8,128)S(1)}, u32[]{:S(2)}, u32[]{:S(2)}) collective-permute-start(f32[16,256]{1,0:T(8,128)S(1)} %select_maximum_fusion), channel_id=1, source_target_pairs={{0,1},{1,2},{2,3},{3,4},{4,5},{5,6},{6,7},{7,8},{8,9},{9,10},{10,1... | collective-permute-start | bytes 49160 | tf_op jit(solution)/shard_map/ppermute | solution.py:29
  40.7 7.0 %collective-permute-done.2 = f32[16,256]{1,0:T(8,128)S(1)} collective-permute-done((f32[16,256]{1,0:T(8,128)S(1)}, f32[16,256]{1,0:T(8,128)S(1)}, u32[]{:S(2)}, u32[]{:S(2)}) %collective-permute-start.2) | collective-permute-done | bytes 16416 | tf_op jit(solution)/shard_map/ppermute | solution.py:29
  48.5 1.9 %collective-permute-start.3 = (f32[8,256]{1,0:T(8,128)S(1)}, f32[8,256]{1,0:T(8,128)S(1)}, u32[]{:S(2)}, u32[]{:S(2)}) collective-permute-start(f32[8,256]{1,0:T(8,128)S(1)} %stack.32), channel_id=1, source_target_pairs={{0,1},{1,0},{2,3},{3,2},{4,5},{5,4},{6,7},{7,6},{8,9},{9,8},{10,11... | collective-permute-start | bytes 24584 | tf_op jit(solution)/shard_map/ppermute | solution.py:29
  53.7 3.3 %all-to-all-start = ((f32[4,8,256]{2,1,0:T(8,128)}), f32[4,8,256]{2,1,0:T(8,128)S(1)}, u32[]{:S(2)}, u32[]{:S(2)}) async-start(f32[4,8,256]{2,1,0:T(8,128)} %broadcast_in_dim.100), calls=%async_computation | async-start | bytes 65536 | tf_op jit(solution)/shard_map/all_to_all | solution.py:37
  57.5 4.8 %all-to-all-done = f32[4,8,256]{2,1,0:T(8,128)S(1)} async-done(((f32[4,8,256]{2,1,0:T(8,128)}), f32[4,8,256]{2,1,0:T(8,128)S(1)}, u32[]{:S(2)}, u32[]{:S(2)}) %all-to-all-start) | async-done | bytes 32800 | tf_op jit(solution)/shard_map/all_to_all | solution.py:37
  63.0 24.4 %all-to-all-start.1 = ((f32[8,8,256]{2,1,0:T(8,128)}), f32[8,8,256]{2,1,0:T(8,128)S(1)}, u32[]{:S(2)}, u32[]{:S(2)}) async-start(f32[8,8,256]{2,1,0:T(8,128)} %broadcast_in_dim.101), calls=%async_computation.1 | async-start | bytes 131072 | tf_op jit(solution)/shard_map/all_to_all | solution.py:37
  89.4 8.9 %all-to-all-done.1 = f32[8,8,256]{2,1,0:T(8,128)S(1)} async-done(((f32[8,8,256]{2,1,0:T(8,128)}), f32[8,8,256]{2,1,0:T(8,128)S(1)}, u32[]{:S(2)}, u32[]{:S(2)}) %all-to-all-start.1) | async-done | bytes 65568 | tf_op jit(solution)/shard_map/all_to_all | solution.py:37
  104.5 1.9 %fusion.21 = f32[256,256]{1,0:T(8,128)} fusion(f32[397,256]{1,0:T(8,128)S(1)} %get-tuple-element.59, f32[397,256]{1,0:T(8,128)S(1)} %get-tuple-element.60, f32[398,256]{1,0:T(8,128)S(1)} %get-tuple-element.55, f32[398,256]{1,0:T(8,128)S(1)} %get-tuple-element.56, f32[399,256]{1,0:T(8,128)S(1)} %get-tuple-element.51, f32[399,256]{1,0:T(8,128)S(1)} %get-tuple-element.52, ...), kind=kOutput, calls=%fused_computation.59 | convolution fusion | flops 315699200 | bytes 3529681 | tf_op jit(solution)/shard_map/dot_general | solution.py:87
  108.3 2.9 %fusion.18 = f32[256,256]{1,0:T(8,128)S(1)} fusion(s32[]{:T(128)S(6)} %select_n.196, f32[8,256]{1,0:T(8,128)S(1)} %copy-done.7, f32[768,256]{1,0:T(8,128)S(1)} %select_bitcast_fusion, f32[8,256]{1,0:T(8,128)S(1)} %broadcast_in_dim.104, f32[397,256]{1,0:T(8,128)} %get-tuple-element.57, f32[397,256]{1,0:T(8,128)} %get-tuple-element.58, ...), kind=kOutput, calls=%fused_computation.38 | convolution fusion | flops 316108800 | bytes 4332502 | tf_op jit(solution)/shard_map/dot_general | solution.py:87
  113.4 2.1 %fusion = f32[256,256]{1,0:T(8,128)S(1)} fusion(f32[784,256]{1,0:T(8,128)S(1)} %get-tuple-element.5, f32[781,256]{1,0:T(8,128)S(1)} %get-tuple-element.17, f32[781,256]{1,0:T(8,128)S(1)} %get-tuple-element.16, f32[782,256]{1,0:T(8,128)S(1)} %get-tuple-element.15, f32[782,256]{1,0:T(8,128)S(1)} %get-tuple-element.14, f32[783,256]{1,0:T(8,128)S(1)} %get-tuple-element.13, ...), kind=kOutput, calls=%fused_computation.12 | convolution fusion | flops 617967616 | bytes 5872704 | tf_op jit(solution)/shard_map/dot_general | solution.py:87
  115.8 2.7 %fusion.50 = f32[256,256]{1,0:T(8,128)S(1)} fusion(f32[397,256]{1,0:T(8,128)S(1)} %copy-done.2, f32[397,256]{1,0:T(8,128)S(1)} %get-tuple-element.22, f32[398,256]{1,0:T(8,128)} %get-tuple-element.21, f32[398,256]{1,0:T(8,128)S(1)} %copy-done.3, f32[399,256]{1,0:T(8,128)} %get-tuple-element.19, f32[399,256]{1,0:T(8,128)} %get-tuple-element.18, ...), kind=kOutput, calls=%fused_computation.90 | convolution fusion | flops 315699200 | bytes 3529681 | tf_op jit(solution)/shard_map/dot_general | solution.py:87
  118.7 1.9 %collective-permute-start.6 = (f32[4,8,16,256]{3,1,2,0:T(8,128)S(1)}, f32[4,8,16,256]{3,1,2,0:T(8,128)S(1)}, u32[]{:S(2)}, u32[]{:S(2)}) collective-permute-start(f32[4,8,16,256]{3,1,2,0:T(8,128)S(1)} %dynamic-slice_bitcast_fusion), channel_id=1, source_target_pairs={{0,1},{1,0},{2,3},{3,2},{4,5},{5,4},{6,7},{7,6},{8,9},{9,8},{10,11... | collective-permute-start | bytes 1572872 | tf_op jit(solution)/shard_map/ppermute | solution.py:29
  120.7 1.9 %collective-permute-done.6 = f32[4,8,16,256]{3,1,2,0:T(8,128)S(1)} collective-permute-done((f32[4,8,16,256]{3,1,2,0:T(8,128)S(1)}, f32[4,8,16,256]{3,1,2,0:T(8,128)S(1)}, u32[]{:S(2)}, u32[]{:S(2)}) %collective-permute-start.6) | collective-permute-done | bytes 524320 | tf_op jit(solution)/shard_map/ppermute | solution.py:29
  122.6 12.5 %all_to_all.20 = f32[4,8,16,256]{3,1,2,0:T(8,128)S(1)} all-to-all(f32[4,8,16,256]{3,1,2,0:T(8,128)S(1)} %bitcast_add_fusion), channel_id=1, replica_groups={{0,16,32,48},{1,17,33,49},{2,18,34,50},{3,19,35,51},{4,20,36,52},{5,21,..., dimensions={0} | all-to-all | bytes 1048576 | tf_op jit(solution)/shard_map/all_to_all | solution.py:37
  135.2 13.9 %all_to_all.21 = f32[8,16,256]{2,1,0:T(8,128)S(1)} all-to-all(f32[8,16,256]{2,1,0:T(8,128)S(1)} %copy.28), channel_id=1, replica_groups={{0,2,4,6,8,10,12,14},{1,3,5,7,9,11,13,15},{16,18,20,22,24,26,28,30},{17..., dimensions={0} | all-to-all | bytes 262144 | tf_op jit(solution)/shard_map/all_to_all | solution.py:37
  149.1 10.8 %collective-permute-start.8 = (f32[8,256]{1,0:T(8,128)S(1)}, f32[8,256]{1,0:T(8,128)S(1)}, u32[]{:S(2)}, u32[]{:S(2)}) collective-permute-start(f32[8,256]{1,0:T(8,128)S(1)} %get-tuple-element.39), channel_id=1, source_target_pairs={{0,64},{1,65},{2,66},{3,67},{4,68},{5,69},{6,70},{7,71},{8,72},{9,... | collective-permute-start | bytes 24584 | tf_op jit(solution)/shard_map/ppermute | solution.py:29
  159.9 4.3 %collective-permute-start.7 = (f32[8,256]{1,0:T(8,128)S(1)}, f32[8,256]{1,0:T(8,128)S(1)}, u32[]{:S(2)}, u32[]{:S(2)}) collective-permute-start(f32[8,256]{1,0:T(8,128)S(1)} %get-tuple-element.38), channel_id=1, source_target_pairs={{0,128},{1,129},{2,130},{3,131},{4,132},{5,133},{6,134},{7,135},{8... | collective-permute-start | bytes 24584 | tf_op jit(solution)/shard_map/ppermute | solution.py:29
  164.3 2.4 %collective-permute-done.7 = f32[8,256]{1,0:T(8,128)S(1)} collective-permute-done((f32[8,256]{1,0:T(8,128)S(1)}, f32[8,256]{1,0:T(8,128)S(1)}, u32[]{:S(2)}, u32[]{:S(2)}) %collective-permute-start.7) | collective-permute-done | bytes 8224 | tf_op jit(solution)/shard_map/ppermute | solution.py:29
  (125 shorter events, 27.9 us)
Async XLA Ops:
  0.0 30.4 %copy-start = (f32[2,768,256]{2,1,0:T(8,128)S(1)}, f32[2,768,256]{2,1,0:T(8,128)}, u32[]{:S(2)}) copy-start(f32[2,768,256]{2,1,0:T(8,128)} %param.7) | copy-start | bytes 4718596
  0.0 27.1 %copy-start.15 = (f32[3,768]{1,0:T(4,128)S(1)}, f32[3,768]{1,0:T(4,128)}, u32[]{:S(2)}) copy-start(f32[3,768]{1,0:T(4,128)} %param.9) | copy-start | bytes 27652
  0.0 27.2 %copy-start.22 = (s32[768]{0:T(1024)S(1)}, s32[768]{0:T(1024)}, u32[]{:S(2)}) copy-start(s32[768]{0:T(1024)} %param.10) | copy-start | bytes 9220
  0.0 27.9 %copy-start.11 = (f32[768]{0:T(1024)S(1)}, f32[768]{0:T(1024)}, u32[]{:S(2)}) copy-start(f32[768]{0:T(1024)} %param.8) | copy-start | bytes 9220
  0.0 30.5 %collective-permute-start.4 = (f32[768,256]{1,0:T(8,128)}, f32[768,256]{1,0:T(8,128)}, u32[]{:S(2)}, u32[]{:S(2)}) collective-permute-start(f32[768,256]{1,0:T(8,128)} %bitcast.42), channel_id=1, source_target_pairs={{64,192},{65,193},{66,194},{67,195},{68,196},{69,197},{70,198},{71... | collective-permute-start | bytes 2359304 | tf_op jit(solution)/shard_map/ppermute | solution.py:29
  10.6 16.6 %copy-start.16 = (f32[256]{0:T(256)}, f32[256]{0:T(256)S(1)}, u32[]{:S(2)}) copy-start(f32[256]{0:T(256)S(1)} %select_reduce_fusion) | copy-start | bytes 3076
  11.9 26.8 %collective-permute-start = (f32[24,256]{1,0:T(8,128)}, f32[24,256]{1,0:T(8,128)}, u32[]{:S(2)}, u32[]{:S(2)}) collective-permute-start(f32[24,256]{1,0:T(8,128)} %pad_maximum_fusion.1), channel_id=1, source_target_pairs={{0,127},{1,64},{2,65},{3,66},{4,67},{5,68},{6,69},{7,70},{8,71},{9... | collective-permute-start | bytes 73736 | tf_op jit(solution)/shard_map/ppermute | solution.py:29
  22.2 82.3 %collective-permute-start.1 = (f32[392,256]{1,0:T(8,128)}, f32[392,256]{1,0:T(8,128)S(1)}, u32[]{:S(2)}, u32[]{:S(2)}) collective-permute-start(f32[392,256]{1,0:T(8,128)} %dynamic-slice_bitcast_fusion.1), channel_id=1, source_target_pairs={{0,64},{1,65},{2,66},{3,67},{4,68},{5,69},{6,70},{7,71},{8,72},{9,... | collective-permute-start | bytes 1204232 | tf_op jit(solution)/shard_map/ppermute | solution.py:29
  27.1 3.2 %copy-start.23 = (s32[3]{0:T(128)}, s32[3]{0:T(128)S(1)}, u32[]{:S(2)}) copy-start(s32[3]{0:T(128)S(1)} %iota_add_fusion) | copy-start | bytes 40
  27.2 3.1 %copy-start.5 = (f32[3,768]{1,0:T(4,128)}, f32[3,768]{1,0:T(4,128)S(1)}, u32[]{:S(2)}) copy-start(f32[3,768]{1,0:T(4,128)S(1)} %compare_select_fusion) | copy-start | bytes 27652
  30.5 2.4 %copy-start.1 = (f32[1,768,256]{2,1,0:T(8,128)S(1)}, f32[1,768,256]{2,1,0:T(8,128)}, u32[]{:S(2)}) copy-start(f32[1,768,256]{2,1,0:T(8,128)} %param.6) | copy-start | bytes 2359300
  30.5 5.4 %copy-start.20 = (f32[3,8]{1,0:T(4,128)S(1)}, f32[3,8]{1,0:T(4,128)}, u32[]{:S(2)}) copy-start(f32[3,8]{1,0:T(4,128)} %slice.246) | copy-start | bytes 292
  32.9 14.9 %collective-permute-start.2 = (f32[16,256]{1,0:T(8,128)S(1)}, f32[16,256]{1,0:T(8,128)S(1)}, u32[]{:S(2)}, u32[]{:S(2)}) collective-permute-start(f32[16,256]{1,0:T(8,128)S(1)} %pad_maximum_fusion.2), channel_id=1, source_target_pairs={{0,385},{1,386},{2,387},{3,388},{4,389},{5,390},{6,391},{7,392},{8... | collective-permute-start | bytes 49160 | tf_op jit(solution)/shard_map/ppermute | solution.py:29
  35.9 14.5 %collective-permute-start.5 = (f32[16,256]{1,0:T(8,128)S(1)}, f32[16,256]{1,0:T(8,128)S(1)}, u32[]{:S(2)}, u32[]{:S(2)}) collective-permute-start(f32[16,256]{1,0:T(8,128)S(1)} %select_maximum_fusion), channel_id=1, source_target_pairs={{0,1},{1,2},{2,3},{3,4},{4,5},{5,6},{6,7},{7,8},{8,9},{9,10},{10,1... | collective-permute-start | bytes 49160 | tf_op jit(solution)/shard_map/ppermute | solution.py:29
  48.5 4.6 %collective-permute-start.3 = (f32[8,256]{1,0:T(8,128)S(1)}, f32[8,256]{1,0:T(8,128)S(1)}, u32[]{:S(2)}, u32[]{:S(2)}) collective-permute-start(f32[8,256]{1,0:T(8,128)S(1)} %stack.32), channel_id=1, source_target_pairs={{0,1},{1,0},{2,3},{3,2},{4,5},{5,4},{6,7},{7,6},{8,9},{9,8},{10,11... | collective-permute-start | bytes 24584 | tf_op jit(solution)/shard_map/ppermute | solution.py:29
  53.7 8.7 %all-to-all-start = ((f32[4,8,256]{2,1,0:T(8,128)}), f32[4,8,256]{2,1,0:T(8,128)S(1)}, u32[]{:S(2)}, u32[]{:S(2)}) async-start(f32[4,8,256]{2,1,0:T(8,128)} %broadcast_in_dim.100), calls=%async_computation | async-start | bytes 65536 | tf_op jit(solution)/shard_map/all_to_all | solution.py:37
  63.0 35.3 %all-to-all-start.1 = ((f32[8,8,256]{2,1,0:T(8,128)}), f32[8,8,256]{2,1,0:T(8,128)S(1)}, u32[]{:S(2)}, u32[]{:S(2)}) async-start(f32[8,8,256]{2,1,0:T(8,128)} %broadcast_in_dim.101), calls=%async_computation.1 | async-start | bytes 131072 | tf_op jit(solution)/shard_map/all_to_all | solution.py:37
  98.3 6.2 %copy-start.13 = (f32[1,256]{1,0:T(1,128)}, f32[1,256]{1,0:T(1,128)S(1)}, u32[]{:S(2)}) copy-start(f32[1,256]{1,0:T(1,128)S(1)} %get-tuple-element.46) | copy-start | bytes 3076
  104.5 3.8 %copy-start.7 = (f32[8,256]{1,0:T(8,128)S(1)}, f32[8,256]{1,0:T(8,128)}, u32[]{:S(2)}) copy-start(f32[8,256]{1,0:T(8,128)} %get-tuple-element.36) | copy-start | bytes 24580
  108.3 3.1 %copy-start.8 = (f32[781]{0:T(1024)S(1)}, f32[781]{0:T(1024)}, u32[]{:S(2)}) copy-start(f32[781]{0:T(1024)} %slice_reduce_fusion) | copy-start | bytes 9376
  115.7 2.9 %copy-start.4 = (f32[1,4,8,2,4,256]{5,2,4,0,1,3:T(8,128)S(1)}, f32[1,4,8,2,4,256]{5,2,4,0,1,3:T(8,128)}, u32[]{:S(2)}) copy-start(f32[1,4,8,2,4,256]{5,2,4,0,1,3:T(8,128)} %copy.27) | copy-start | bytes 786436
  118.7 3.8 %collective-permute-start.6 = (f32[4,8,16,256]{3,1,2,0:T(8,128)S(1)}, f32[4,8,16,256]{3,1,2,0:T(8,128)S(1)}, u32[]{:S(2)}, u32[]{:S(2)}) collective-permute-start(f32[4,8,16,256]{3,1,2,0:T(8,128)S(1)} %dynamic-slice_bitcast_fusion), channel_id=1, source_target_pairs={{0,1},{1,0},{2,3},{3,2},{4,5},{5,4},{6,7},{7,6},{8,9},{9,8},{10,11... | collective-permute-start | bytes 1572872 | tf_op jit(solution)/shard_map/ppermute | solution.py:29
  149.1 15.2 %collective-permute-start.8 = (f32[8,256]{1,0:T(8,128)S(1)}, f32[8,256]{1,0:T(8,128)S(1)}, u32[]{:S(2)}, u32[]{:S(2)}) collective-permute-start(f32[8,256]{1,0:T(8,128)S(1)} %get-tuple-element.39), channel_id=1, source_target_pairs={{0,64},{1,65},{2,66},{3,67},{4,68},{5,69},{6,70},{7,71},{8,72},{9,... | collective-permute-start | bytes 24584 | tf_op jit(solution)/shard_map/ppermute | solution.py:29
  159.9 6.8 %collective-permute-start.7 = (f32[8,256]{1,0:T(8,128)S(1)}, f32[8,256]{1,0:T(8,128)S(1)}, u32[]{:S(2)}, u32[]{:S(2)}) collective-permute-start(f32[8,256]{1,0:T(8,128)S(1)} %get-tuple-element.38), channel_id=1, source_target_pairs={{0,128},{1,129},{2,130},{3,131},{4,132},{5,133},{6,134},{7,135},{8... | collective-permute-start | bytes 24584 | tf_op jit(solution)/shard_map/ppermute | solution.py:29
  (12 other events, 16.6 us)

commit v2 on v1

v2 whole, which is shorter than its diff:
```python
import jax
import jax.numpy as jnp
from jax import lax
from jax.experimental import pallas as pl
from jax.experimental.pallas import tpu as pltpu
from jax.sharding import PartitionSpec as P

radial_step = 0.5
edge = 8
both = ("rho", "basis")
exact = lax.Precision.HIGHEST


def hops(target):
    pairs = []
    for rho in range(8):
        for basis in range(64):
            to = target(rho // 2, rho % 2, basis // 16, basis // 2 % 8, basis % 2)
            if to is not None:
                y, h, x, z, core = to
                pairs.append((rho * 64 + basis, (y * 2 + h) * 64 + x * 16 + z * 2 + core))
    return pairs


def basis_step(x, z, core, by):
    index = (x * 16 + z * 2 + core + by) % 64
    return index // 16, index // 2 % 8, index % 2


def move(array, target):
    return lax.ppermute(array, both, hops(target))


def ring(xs, zs, cores):
    return [x * 16 + z * 2 + core for x in xs for z in zs for core in cores]


quarters = (range(4), range(4, 8))
x_groups = [ring(range(4), (z,), (core,)) for z in range(8) for core in range(2)]
z_groups = [ring((x,), q, (core,)) for x in range(4) for q in quarters for core in range(2)]
cube_groups = [ring(range(4), q, range(2)) for q in quarters]


def spread(array, groups):
    return lax.all_to_all(array, "basis", 0, 0, axis_index_groups=groups)


def swap_core(y, h, x, z, core):
    return y, h, x, z, 1 - core


def swap_quarter(y, h, x, z, core):
    return y, h, x, z ^ 4, core


def swap_parity(y, h, x, z, core):
    return y, 1 - h, x, z, core


def swap_both(y, h, x, z, core):
    return y, 1 - h, x, z ^ 4, core


def to_neighbour(y, h, x, z, core):
    to = y - 1 if h == 0 else y + 1
    return (to, h, x, z, core) if 0 <= to < 4 else None


def from_neighbour(y, h, x, z, core):
    to = y + 1 if h == 0 else y - 1
    return (to, h, x, z, core) if 0 <= to < 4 else None


def halo_own(y, h, x, z, core):
    return (y, h, *basis_step(x, z, core, 1 if h == 0 else -1))


def halo_visitor(y, h, x, z, core):
    return (y, 1 - h, *basis_step(x, z, core, -1 if h == 0 else 1))


def halo_neighbour(y, h, x, z, core):
    to = y - 1 if h == 0 else y + 1
    return (to, h, *basis_step(x, z, core, 1 if h == 0 else -1)) if 0 <= to < 4 else None


def product(a, b):
    return lax.dot_general(
        a, b, (((0,), (0,)), ((), ())), precision=exact, preferred_element_type=jnp.float32
    )


def sign_of(values):
    return jnp.where(values > 0.0, 1.0, jnp.where(values < 0.0, -1.0, 0.0))


def place():
    rho, basis = lax.axis_index("rho"), lax.axis_index("basis")
    return lax.div(rho, 2), lax.rem(rho, 2), basis


def prepare(own, ends_first, ends_last, band, reach, rows_of, out_half, out_rim, out_visitor, out_picked):
    y, h, basis = place()
    rows, width = own.shape
    half = rows // 2
    out_half[...] = own[pl.ds(pl.multiple_of((1 - h) * (half - edge), edge), half + edge), :]
    spot = rows_of[...] - basis * rows
    step = 64
    picked = jnp.zeros((edge, width), jnp.float32)
    for start in range(0, rows, step):
        line = lax.broadcasted_iota(jnp.int32, (step, width), 0) + start
        hit = jnp.where(line == spot, own[start : start + step, :], 0.0)
        picked = picked + hit.reshape(step // edge, edge, width).sum(0)
    picked = jnp.broadcast_to(picked.sum(0, keepdims=True), (edge, width))
    out_picked[...] = jnp.broadcast_to(picked[None], out_picked.shape)
    even = h == 0
    depth = lax.broadcasted_iota(jnp.int32, band.shape, 0) + 1
    masked = jnp.where(depth <= reach[...], band[...], 0.0)
    out_rim[0:edge, :] = jnp.where(even, own[rows - edge :, :], own[:edge, :])
    out_rim[edge : 2 * edge, :] = jnp.zeros((edge, width), jnp.float32)
    out_rim[edge : edge + band.shape[0], :] = masked[:, rows - width :]
    out_rim[2 * edge :, :] = jnp.where(even, ends_last[1], ends_first[0])
    out_visitor[0:edge, :] = own[rows - edge :, :]
    out_visitor[edge:, :] = ends_last[0]


def apply(own, near, ends, own_rim, near_rim, own_sum, near_sum, diag, band, reach,
          out_slope, out_own, out_near, out_curve, own_f, near_f, slope_f, weight_f, turned, applied_f, own_w, near_w, slope_w, weight_w):
    y, h, basis = place()
    rows, width = own.shape
    half = rows // 2
    pad = 2 * edge
    frame = rows + 2 * pad
    even = h == 0
    at_far = (even & (y == 3)) | ((h == 1) & (y == 0))
    far = 1 - h
    own_sign = sign_of(own_sum[0:1, :])
    near_sign = sign_of(near_sum[0:1, :])
    has_low = (even & (basis > 0)).astype(jnp.float32)
    has_high = ((h == 1) & (basis < 63)).astype(jnp.float32)
    blank = jnp.zeros((pad, width), jnp.float32)
    for field in (own_f, near_f):
        field[0:pad, :] = blank
        field[pad + rows :, :] = blank
    own_f[pad : pad + rows, :] = own[...] * own_sign
    own_f[edge:pad, :] = own_rim[0:edge, :] * own_sign * has_low
    own_f[pad + rows : pad + rows + edge, :] = own_rim[0:edge, :] * own_sign * has_high

    @pl.when(at_far)
    def _():
        near_f[pad : pad + rows, :] = ends[far]
        near_f[edge:pad, :] = own_rim[2 * edge :, :] * has_low
        near_f[pad + rows : pad + rows + edge, :] = own_rim[2 * edge :, :] * has_high

    @pl.when(jnp.logical_not(at_far))
    def _():
        near_f[pad : pad + rows, :] = near[...] * near_sign
        near_f[edge:pad, :] = near_rim[0:edge, :] * near_sign * has_low
        near_f[pad + rows : pad + rows + edge, :] = near_rim[0:edge, :] * near_sign * has_high

    turn = jnp.where(even, 1.0, -1.0)
    slope_f[...] = (near_f[...] - own_f[...]) * turn / (2.0 * radial_step)

    count = band.shape[0]
    depth = lax.broadcasted_iota(jnp.int32, band.shape, 0) + 1
    masked = jnp.where(depth <= reach[...], band[...], 0.0)
    lanes = 128
    turned[...] = jnp.zeros(turned.shape, jnp.float32)
    turned[0:1, :] = diag[...]
    turned[edge : edge + count, :] = masked
    weight_f[...] = jnp.zeros(weight_f.shape, jnp.float32)
    for start in range(0, rows, lanes):
        weight_f[pad + start : pad + start + lanes, :] = turned[:, start : start + lanes].T
    before = own_rim[edge : 2 * edge, width - lanes :]
    lane = lax.broadcasted_iota(jnp.int32, before.shape, 1)
    level = lax.broadcasted_iota(jnp.int32, before.shape, 0) + 1
    before = jnp.where(lane + level >= lanes, before, 0.0) * has_low
    turned[edge : 2 * edge, 0:lanes] = before
    turned[0:edge, 0:lanes] = jnp.zeros((edge, lanes), jnp.float32)
    weight_f[edge:pad, :] = turned[:, 0:lanes].T[lanes - edge :, :]

    def banded(field, weight, start, size):
        total = weight[start : start + size, 0:1] * field[start : start + size, :]
        for d in range(1, count + 1):
            col = edge + d - 1
            total = total + weight[start : start + size, col : col + 1] * field[start + d : start + d + size, :]
            total = total + weight[start - d : start - d + size, col : col + 1] * field[start - d : start - d + size, :]
        return total

    step = 16
    for start in range(edge, frame - edge, step):
        applied_f[start - edge : start - edge + step, :] = banded(slope_f, weight_f, start, step)
    out_curve[...] = product(slope_f[edge : frame - edge, :], applied_f[...])

    window = half + 2 * pad
    base = pl.multiple_of(h * half, edge)
    line = lax.broadcasted_iota(jnp.int32, (window, width), 0)
    weight_w[...] = weight_f[pl.ds(base, window), :]
    keep = (line >= jnp.where(even, pad, 0)) & (line < jnp.where(even, pad + half, window))
    for field, held in ((own_f, own_w), (near_f, near_w), (slope_f, slope_w)):
        held[...] = jnp.where(keep, field[pl.ds(base, window), :], 0.0)
    size = half + 2 * edge
    step = 16
    for held, out in ((own_w, out_own), (near_w, out_near), (slope_w, out_slope)):
        for start in range(0, size, step):
            line = lax.broadcasted_iota(jnp.int32, (step, width), 0) + start
            inside = (line >= jnp.where(even, 0, edge)) & (line < jnp.where(even, size, edge + half))
            out[start : start + step, :] = jnp.where(inside, banded(held, weight_w, start + edge, step), 0.0)


def multiply(visitor, visitor_rim, visitor_sum, ends, slope_applied, own_applied, near_applied, curve,
             out_keep, out_send, seen, moved):
    y, h, basis = place()
    even = h == 0
    core = lax.rem(basis, 2)
    rows = ends.shape[1]
    half = rows // 2
    size = half + edge
    at_near = (even & (y == 0)) | ((h == 1) & (y == 3))
    at = pl.multiple_of(jnp.where(even, edge, 0), edge)
    visitor_sign = sign_of(visitor_sum[0:1, :])
    seen[0:edge, :] = visitor_rim[0:edge, :] * visitor_sign
    seen[size:, :] = visitor_rim[0:edge, :] * visitor_sign
    seen[pl.ds(at, size), :] = visitor[...] * visitor_sign
    moved[...] = seen[...]

    @pl.when(at_near)
    def _():
        moved[0:edge, :] = moved[0:edge, :] - visitor_rim[edge : 2 * edge, :]
        beside = ends[h, pl.ds(pl.multiple_of(h * (half - edge), edge), size), :]
        moved[pl.ds(at, size), :] = seen[pl.ds(at, size), :] - beside

    scale = 1.0 / (2.0 * radial_step)
    cross = product(seen[...], slope_applied[...])
    first = product(own_applied[...], moved[...] * scale)
    second = product(near_applied[...], seen[...] * scale)
    low = core == 0
    for index, part in enumerate((cross, curve[...], first, second)):
        part = part.reshape(32, 2 * 4, part.shape[1])
        front, back = part[:, :4, :], part[:, 4:, :]
        out_keep[:, 4 * index : 4 * index + 4, :] = jnp.where(low, front, back)
        out_send[:, 4 * index : 4 * index + 4, :] = jnp.where(low, back, front)


def kernel(body, shapes, scratch, work, *operands, in_specs=None):
    extra = {} if in_specs is None else {"in_specs": in_specs}
    return pl.pallas_call(
        body,
        out_shape=[jax.ShapeDtypeStruct(shape, jnp.float32) for shape in shapes],
        scratch_shapes=[pltpu.VMEM(shape, jnp.float32) for shape in scratch],
        compiler_params=pltpu.CompilerParams(vmem_limit_bytes=40 * 1024 * 1024),
        cost_estimate=pl.CostEstimate(flops=work, bytes_accessed=4 * 1024 * 1024, transcendentals=0),
        **extra,
    )(*operands)


def shards(panels, end_panels, correlation_diag, correlation_band, band_reach, sign_rows):
    own = panels[0]
    rows, width = own.shape
    half = rows // 2
    rho, basis = lax.axis_index("rho"), lax.axis_index("basis")
    h, quarter = rho % 2, basis // 8 % 2
    reach = band_reach[None, :]

    half_rows, rim, visitor_rim, picked = kernel(
        prepare,
        [(half + edge, width), (3 * edge, width), (2 * edge, width), (32, edge, width)],
        [],
        1000000,
        own,
        end_panels[:, :edge],
        end_panels[:, rows - edge :],
        correlation_band,
        reach,
        sign_rows,
    )
    visitor = move(half_rows, swap_parity)
    picked = spread(picked, cube_groups).sum(0)
    near = move(own, to_neighbour)
    own_rim = move(rim, halo_own)
    near_rim = move(rim, halo_neighbour)
    visitor_rim = move(visitor_rim, halo_visitor)
    own_sum = picked + move(picked, swap_quarter)
    near_sum = move(own_sum, to_neighbour)
    visitor_sum = move(own_sum, swap_both)

    window = half + 4 * edge
    frame = rows + 4 * edge
    slope_applied, own_applied, near_applied, curve = kernel(
        apply,
        [(half + 2 * edge, width)] * 3 + [(width, width)],
        [(frame, width)] * 3
        + [(frame, 2 * edge), (2 * edge, rows), (frame - 2 * edge, width)]
        + [(window, width)] * 3
        + [(window, 2 * edge)],
        1000000000,
        own, near, end_panels, own_rim, near_rim, own_sum, near_sum, correlation_diag[None, :], correlation_band, reach,
    )
    keep, send = kernel(
        multiply,
        [(32, 16, width)] * 2,
        [(half + 2 * edge, width)] * 2,
        1000000000,
        visitor, visitor_rim, visitor_sum, end_panels, slope_applied, own_applied, near_applied, curve,
    )
    mine = keep + move(send, swap_core)
    mine = spread(mine.reshape(4, 8, 16, width), x_groups).sum(0)
    mine = spread(mine.reshape(2, 4, 16, width).transpose(1, 0, 2, 3), z_groups).sum(0)
    here = quarter == 0
    low, high = mine[0], mine[1]
    stay = jnp.where(here, low, high)
    go = jnp.where(here, high, low)
    mine = jnp.concatenate([go[:8], stay[8:]]) + move(jnp.concatenate([stay[:8], go[8:]]), swap_quarter)
    away = move(mine[:8], swap_both)
    second = move(mine[8:], from_neighbour)[4:]
    turn = jnp.where(h == 0, 1.0, -1.0)
    drift = turn * (mine[8:12] - second) + away[:4]
    return jnp.stack([drift, away[4:]], axis=1)[:, None]


def solution(mesh):
    in_specs = (
        P("rho", "basis", None),
        P(None, "basis", None),
        P("basis"),
        P(None, "basis"),
        P("basis"),
        P("rho", None),
    )
    out_specs = P("basis", "rho", None, None)
    return jax.shard_map(shards, mesh=mesh, in_specs=in_specs, out_specs=out_specs, check_vma=False)
```

time: 168 us -> 143 us (0.85)
  waiting for transfers between devices: 25.1 us -> 51.4 us
  other arithmetic: 14.7 us -> 0.81 us
  blocking collectives: 26.4 us -> 14.1 us
  local copies, waits for them, and re-layouts: 17.3 us -> 6.07 us
  starting transfers between devices: 73.7 us -> 63 us
  matrix products: 9.59 us -> 0 us
  Pallas kernels: 0 us -> 6.74 us
    ppermute x9 -> x12, waiting for transfers between devices: 11.3 us -> 45.5 us  [move(): return lax.ppermute(array, both, hops(target))]
    all_to_all x2 -> x1, blocking collectives: 26.4 us -> 14.1 us  [spread(): return lax.all_to_all(array, 'basis', 0, 0, axis_index_groups=groups)]
    all_to_all x2, starting transfers between devices: 27.7 us -> 16.5 us  [spread(): return lax.all_to_all(array, 'basis', 0, 0, axis_index_groups=groups)]
    dot_general x4 -> x0, matrix products: 9.59 us -> none  [product(): return lax.dot_general(a, b, (((0,), (0,)), ((), ())), precision=exact)]
    all_to_all x2, waiting for transfers between devices: 13.7 us -> 5.92 us  [spread(): return lax.all_to_all(array, 'basis', 0, 0, axis_index_groups=groups)]
    pallas_call x0 -> x3, Pallas kernels: none -> 6.74 us  [kernel(): pl.pallas_call(body, out_shape=[jax.ShapeDtypeStruct(shape, jnp.float32)...]
    slice x12 -> x3, local copies, waits for them, and re-layouts: 7.18 us -> 0.77 us  [the longest x1 0.76 us: shards(): end_panels[:, rows - edge:]]
    select_n x9 -> x1, other arithmetic: 4.7 us -> 0.01 us  [shards(): stay = jnp.where(here, low, high)]
  transfers between devices with their start and end apart: 11 -> 14, of which waited for: 5 -> 6; matrix products, arithmetic and copies ran while one was open for 16% -> 0% of each run, Pallas kernels for 0% -> 3%
where the time goes in v2:
time: 143 us; the launch traced here: 142 us
  starting transfers between devices  63 us (44%)
  waiting for transfers between devices  51.4 us (36%)
  blocking collectives  14.1 us (10%)
  Pallas kernels  6.74 us (5%)
  local copies, waits for them, and re-layouts  6.07 us (4%)
    ppermute x12, starting transfers between devices, move(): return lax.ppermute(array, both, hops(target))  46.5 us
    ppermute x12, waiting for transfers between devices, move(): return lax.ppermute(array, both, hops(target))  45.5 us
    all_to_all x2, starting transfers between devices, spread(): return lax.all_to_all(array, 'basis', 0, 0, axis_index_groups=groups)  16.5 us
    all_to_all x1, blocking collectives, spread(): return lax.all_to_all(array, 'basis', 0, 0, axis_index_groups=groups)  14.1 us
    pallas_call x3, Pallas kernels, kernel(): pl.pallas_call(body, out_shape=[jax.ShapeDtypeStruct(shape, jnp.float32)...  6.74 us
    all_to_all x2, waiting for transfers between devices, spread(): return lax.all_to_all(array, 'basis', 0, 0, axis_index_groups=groups)  5.92 us
    unnamed x14, local copies, waits for them, and re-layouts  3.93 us
  transfers between devices with their start and end apart: 14, of which 6 were waited for; matrix products, arithmetic and copies ran while one was open for 0% of the time, Pallas kernels for 3%

profile of v2, /device:TPU:8, one launch (start us, length us, event | category | flops | bytes accessed | tf_op | source)
XLA Modules:
  0.0 142.4 jit_solution(18017649825783353252)
XLA Ops:
  4.8 8.7 %all-to-all-start = ((f32[32,8,256]{2,1,0:T(8,128)}), f32[32,8,256]{2,1,0:T(8,128)S(1)}, u32[]{:S(2)}, u32[]{:S(2)}) async-start(f32[32,8,256]{2,1,0:T(8,128)} %get-tuple-element.17), calls=%async_computation | async-start | bytes 524288 | tf_op jit(solution)/shard_map/all_to_all | solution.py:45
  13.6 2.9 %collective-permute-start.4 = (f32[768,256]{1,0:T(8,128)}, f32[768,256]{1,0:T(8,128)S(1)}, u32[]{:S(2)}, u32[]{:S(2)}) collective-permute-start(f32[768,256]{1,0:T(8,128)} %bitcast.17), channel_id=1, source_target_pairs={{64,192},{65,193},{66,194},{67,195},{68,196},{69,197},{70,198},{71... | collective-permute-start | bytes 2359304 | tf_op jit(solution)/shard_map/ppermute | solution.py:31
  16.4 13.7 %collective-permute-start = (f32[392,256]{1,0:T(8,128)S(1)}, f32[392,256]{1,0:T(8,128)S(1)}, u32[]{:S(2)}, u32[]{:S(2)}) collective-permute-start(f32[392,256]{1,0:T(8,128)S(1)} %get-tuple-element.15), channel_id=1, source_target_pairs={{0,64},{1,65},{2,66},{3,67},{4,68},{5,69},{6,70},{7,71},{8,72},{9,... | collective-permute-start | bytes 1204232 | tf_op jit(solution)/shard_map/ppermute | solution.py:31
  30.1 1.9 %collective-permute-start.5 = (f32[24,256]{1,0:T(8,128)S(1)}, f32[24,256]{1,0:T(8,128)S(1)}, u32[]{:S(2)}, u32[]{:S(2)}) collective-permute-start(f32[24,256]{1,0:T(8,128)S(1)} %get-tuple-element.18), channel_id=1, source_target_pairs={{0,1},{1,2},{2,3},{3,4},{4,5},{5,6},{6,7},{7,8},{8,9},{9,10},{10,1... | collective-permute-start | bytes 73736 | tf_op jit(solution)/shard_map/ppermute | solution.py:31
  32.0 3.9 %collective-permute-start.6 = (f32[24,256]{1,0:T(8,128)S(1)}, f32[24,256]{1,0:T(8,128)S(1)}, u32[]{:S(2)}, u32[]{:S(2)}) collective-permute-start(f32[24,256]{1,0:T(8,128)S(1)} %get-tuple-element.18), channel_id=1, source_target_pairs={{64,255},{65,192},{66,193},{67,194},{68,195},{69,196},{70,197},{71... | collective-permute-start | bytes 73736 | tf_op jit(solution)/shard_map/ppermute | solution.py:31
  36.0 4.3 %collective-permute-start.2 = (f32[8,256]{1,0:T(8,128)S(1)}, f32[8,256]{1,0:T(8,128)S(1)}, u32[]{:S(2)}, u32[]{:S(2)}) collective-permute-start(f32[8,256]{1,0:T(8,128)S(1)} %reduce_sum.27), channel_id=1, source_target_pairs={{0,8},{1,9},{2,10},{3,11},{4,12},{5,13},{6,14},{7,15},{8,0},{9,1},... | collective-permute-start | bytes 24584 | tf_op jit(solution)/shard_map/ppermute | solution.py:31
  40.3 28.2 %collective-permute-done.2 = f32[8,256]{1,0:T(8,128)S(1)} collective-permute-done((f32[8,256]{1,0:T(8,128)S(1)}, f32[8,256]{1,0:T(8,128)S(1)}, u32[]{:S(2)}, u32[]{:S(2)}) %collective-permute-start.2) | collective-permute-done | bytes 8224 | tf_op jit(solution)/shard_map/ppermute | solution.py:31
  68.5 1.9 %collective-permute-start.7 = (f32[8,256]{1,0:T(8,128)S(1)}, f32[8,256]{1,0:T(8,128)S(1)}, u32[]{:S(2)}, u32[]{:S(2)}) collective-permute-start(f32[8,256]{1,0:T(8,128)S(1)} %add.22.own_sum), channel_id=1, source_target_pairs={{64,192},{65,193},{66,194},{67,195},{68,196},{69,197},{70,198},{71... | collective-permute-start | bytes 24584 | tf_op jit(solution)/shard_map/ppermute | solution.py:31
  70.4 1.9 %collective-permute-start.1 = (f32[16,256]{1,0:T(8,128)S(1)}, f32[16,256]{1,0:T(8,128)S(1)}, u32[]{:S(2)}, u32[]{:S(2)}) collective-permute-start(f32[16,256]{1,0:T(8,128)S(1)} %get-tuple-element.16), channel_id=1, source_target_pairs={{0,127},{1,64},{2,65},{3,66},{4,67},{5,68},{6,69},{7,70},{8,71},{9... | collective-permute-start | bytes 49160 | tf_op jit(solution)/shard_map/ppermute | solution.py:31
  72.4 1.9 %collective-permute-start.3 = (f32[8,256]{1,0:T(8,128)S(1)}, f32[8,256]{1,0:T(8,128)S(1)}, u32[]{:S(2)}, u32[]{:S(2)}) collective-permute-start(f32[8,256]{1,0:T(8,128)S(1)} %add.22.own_sum), channel_id=1, source_target_pairs={{0,72},{1,73},{2,74},{3,75},{4,76},{5,77},{6,78},{7,79},{8,64},{9,... | collective-permute-start | bytes 24584 | tf_op jit(solution)/shard_map/ppermute | solution.py:31
  74.4 1.4 copy-done.5
  75.8 4.1 %shard_map.65 = (f32[400,256]{1,0:T(8,128)S(1)}, f32[400,256]{1,0:T(8,128)S(1)}, f32[400,256]{1,0:T(8,128)S(1)}, f32[256,256]{1,0:T(8,128)S(1)}) custom-call(f32[768,256]{1,0:T(8,128)S(1)} %bitcast.19, f32[768,256]{1,0:T(8,128)S(1)} %collective-permute-done.4.near, f32[2,768,256]{2,1,0:T(8,128)S(1)} %copy-done.5, ...), custom_call_target="tpu_custom_call" | custom-call | flops 1000000000 | bytes 4194304 | tf_op jit(solution)/shard_map/pallas_call | solution.py:247
  79.9 1.9 %collective-permute-done.3.visitor_sum = f32[8,256]{1,0:T(8,128)S(1)} collective-permute-done((f32[8,256]{1,0:T(8,128)S(1)}, f32[8,256]{1,0:T(8,128)S(1)}, u32[]{:S(2)}, u32[]{:S(2)}) %collective-permute-start.3) | collective-permute-done | bytes 8224 | tf_op jit(solution)/shard_map/ppermute | solution.py:31
  81.8 1.8 %shard_map.66 = (f32[32,16,256]{2,1,0:T(8,128)S(1)}, f32[32,16,256]{2,1,0:T(8,128)S(1)}) custom-call(f32[392,256]{1,0:T(8,128)S(1)} %collective-permute-done.visitor, f32[16,256]{1,0:T(8,128)S(1)} %collective-permute-done.1.visitor_rim, f32[8,256]{1,0:T(8,128)S(1)} %collective-permute-done.3.visitor_sum, f32[2,768,256]{2,1,0:T(8,128)S(1)} %copy-done.5, ...), custom_call_target="tpu_custom_call" | custom-call | flops 1000000000 | bytes 4194304 | tf_op jit(solution)/shard_map/pallas_call | solution.py:247
  83.6 5.4 %collective-permute-start.8 = (f32[32,16,256]{2,1,0:T(8,128)S(1)}, f32[32,16,256]{2,1,0:T(8,128)S(1)}, u32[]{:S(2)}, u32[]{:S(2)}) collective-permute-start(f32[32,16,256]{2,1,0:T(8,128)S(1)} %get-tuple-element.24), channel_id=1, source_target_pairs={{0,1},{1,0},{2,3},{3,2},{4,5},{5,4},{6,7},{7,6},{8,9},{9,8},{10,11... | collective-permute-start | bytes 1572872 | tf_op jit(solution)/shard_map/ppermute | solution.py:31
  89.0 1.5 %collective-permute-done.8 = f32[32,16,256]{2,1,0:T(8,128)S(1)} collective-permute-done((f32[32,16,256]{2,1,0:T(8,128)S(1)}, f32[32,16,256]{2,1,0:T(8,128)S(1)}, u32[]{:S(2)}, u32[]{:S(2)}) %collective-permute-start.8) | collective-permute-done | bytes 524320 | tf_op jit(solution)/shard_map/ppermute | solution.py:31
  90.6 14.1 %all_to_all.15 = f32[4,8,16,256]{3,2,1,0:T(8,128)S(1)} all-to-all(f32[4,8,16,256]{3,2,1,0:T(8,128)S(1)} %bitcast.20), channel_id=1, replica_groups={{0,16,32,48},{1,17,33,49},{2,18,34,50},{3,19,35,51},{4,20,36,52},{5,21,..., dimensions={0} | all-to-all | bytes 1048576 | tf_op jit(solution)/shard_map/all_to_all | solution.py:45
  105.4 7.7 %all-to-all-start.2 = ((f32[4,2,16,256]{3,2,1,0:T(8,128)}), f32[4,2,16,256]{3,2,1,0:T(8,128)S(1)}, u32[]{:S(2)}, u32[]{:S(2)}) async-start(f32[4,2,16,256]{3,2,1,0:T(8,128)} %copy.9), calls=%async_computation.2 | async-start | bytes 262144 | tf_op jit(solution)/shard_map/all_to_all | solution.py:45
  113.2 5.9 %all-to-all-done.2 = f32[4,2,16,256]{3,2,1,0:T(8,128)S(1)} async-done(((f32[4,2,16,256]{3,2,1,0:T(8,128)}), f32[4,2,16,256]{3,2,1,0:T(8,128)S(1)}, u32[]{:S(2)}, u32[]{:S(2)}) %all-to-all-start.2) | async-done | bytes 131104 | tf_op jit(solution)/shard_map/all_to_all | solution.py:45
  119.2 3.0 %collective-permute-start.9 = (f32[16,256]{1,0:T(8,128)S(1)}, f32[16,256]{1,0:T(8,128)S(1)}, u32[]{:S(2)}, u32[]{:S(2)}) collective-permute-start(f32[16,256]{1,0:T(8,128)S(1)} %pad_maximum_fusion), channel_id=1, source_target_pairs={{0,8},{1,9},{2,10},{3,11},{4,12},{5,13},{6,14},{7,15},{8,0},{9,1},... | collective-permute-start | bytes 49160 | tf_op jit(solution)/shard_map/ppermute | solution.py:31
  122.2 6.5 %collective-permute-done.9 = f32[16,256]{1,0:T(8,128)S(1)} collective-permute-done((f32[16,256]{1,0:T(8,128)S(1)}, f32[16,256]{1,0:T(8,128)S(1)}, u32[]{:S(2)}, u32[]{:S(2)}) %collective-permute-start.9) | collective-permute-done | bytes 16416 | tf_op jit(solution)/shard_map/ppermute | solution.py:31
  128.7 3.6 %collective-permute-start.10 = (f32[8,256]{1,0:T(8,128)S(1)}, f32[8,256]{1,0:T(8,128)S(1)}, u32[]{:S(2)}, u32[]{:S(2)}) collective-permute-start(f32[8,256]{1,0:T(8,128)S(1)} %get-tuple-element.29), channel_id=1, source_target_pairs={{0,128},{1,129},{2,130},{3,131},{4,132},{5,133},{6,134},{7,135},{8... | collective-permute-start | bytes 24584 | tf_op jit(solution)/shard_map/ppermute | solution.py:31
  132.3 2.1 %collective-permute-start.11 = (f32[8,256]{1,0:T(8,128)S(1)}, f32[8,256]{1,0:T(8,128)S(1)}, u32[]{:S(2)}, u32[]{:S(2)}) collective-permute-start(f32[8,256]{1,0:T(8,128)S(1)} %get-tuple-element.30), channel_id=1, source_target_pairs={{0,72},{1,73},{2,74},{3,75},{4,76},{5,77},{6,78},{7,79},{8,64},{9,... | collective-permute-start | bytes 24584 | tf_op jit(solution)/shard_map/ppermute | solution.py:31
  134.5 7.3 %collective-permute-done.11 = f32[8,256]{1,0:T(8,128)S(1)} collective-permute-done((f32[8,256]{1,0:T(8,128)S(1)}, f32[8,256]{1,0:T(8,128)S(1)}, u32[]{:S(2)}, u32[]{:S(2)}) %collective-permute-start.11) | collective-permute-done | bytes 8224 | tf_op jit(solution)/shard_map/ppermute | solution.py:31
  (40 shorter events, 6.3 us)
Async XLA Ops:
  0.0 74.3 %copy-start.3 = (f32[3,768]{1,0:T(4,128)S(1)}, f32[3,768]{1,0:T(4,128)}, u32[]{:S(2)}) copy-start(f32[3,768]{1,0:T(4,128)} %band.3) | copy-start | bytes 27652
  0.0 70.4 %copy-start.6 = (f32[768]{0:T(1024)S(1)}, f32[768]{0:T(1024)}, u32[]{:S(2)}) copy-start(f32[768]{0:T(1024)} %param.8) | copy-start | bytes 9220
  1.5 1.1 copy-start
  2.6 0.7 copy-start.2
  3.3 0.7 copy-start.4
  4.0 70.4 %copy-start.1 = (f32[1,768,256]{2,1,0:T(8,128)S(1)}, f32[1,768,256]{2,1,0:T(8,128)}, u32[]{:S(2)}) copy-start(f32[1,768,256]{2,1,0:T(8,128)} %param.6) | copy-start | bytes 2359300
  4.8 31.1 %all-to-all-start = ((f32[32,8,256]{2,1,0:T(8,128)}), f32[32,8,256]{2,1,0:T(8,128)S(1)}, u32[]{:S(2)}, u32[]{:S(2)}) async-start(f32[32,8,256]{2,1,0:T(8,128)} %get-tuple-element.17), calls=%async_computation | async-start | bytes 524288 | tf_op jit(solution)/shard_map/all_to_all | solution.py:45
  13.6 60.7 %collective-permute-start.4 = (f32[768,256]{1,0:T(8,128)}, f32[768,256]{1,0:T(8,128)S(1)}, u32[]{:S(2)}, u32[]{:S(2)}) collective-permute-start(f32[768,256]{1,0:T(8,128)} %bitcast.17), channel_id=1, source_target_pairs={{64,192},{65,193},{66,194},{67,195},{68,196},{69,197},{70,198},{71... | collective-permute-start | bytes 2359304 | tf_op jit(solution)/shard_map/ppermute | solution.py:31
  16.4 63.5 %collective-permute-start = (f32[392,256]{1,0:T(8,128)S(1)}, f32[392,256]{1,0:T(8,128)S(1)}, u32[]{:S(2)}, u32[]{:S(2)}) collective-permute-start(f32[392,256]{1,0:T(8,128)S(1)} %get-tuple-element.15), channel_id=1, source_target_pairs={{0,64},{1,65},{2,66},{3,67},{4,68},{5,69},{6,70},{7,71},{8,72},{9,... | collective-permute-start | bytes 1204232 | tf_op jit(solution)/shard_map/ppermute | solution.py:31
  30.1 40.3 %collective-permute-start.5 = (f32[24,256]{1,0:T(8,128)S(1)}, f32[24,256]{1,0:T(8,128)S(1)}, u32[]{:S(2)}, u32[]{:S(2)}) collective-permute-start(f32[24,256]{1,0:T(8,128)S(1)} %get-tuple-element.18), channel_id=1, source_target_pairs={{0,1},{1,2},{2,3},{3,4},{4,5},{5,6},{6,7},{7,8},{8,9},{9,10},{10,1... | collective-permute-start | bytes 73736 | tf_op jit(solution)/shard_map/ppermute | solution.py:31
  32.0 40.4 %collective-permute-start.6 = (f32[24,256]{1,0:T(8,128)S(1)}, f32[24,256]{1,0:T(8,128)S(1)}, u32[]{:S(2)}, u32[]{:S(2)}) collective-permute-start(f32[24,256]{1,0:T(8,128)S(1)} %get-tuple-element.18), channel_id=1, source_target_pairs={{64,255},{65,192},{66,193},{67,194},{68,195},{69,196},{70,197},{71... | collective-permute-start | bytes 73736 | tf_op jit(solution)/shard_map/ppermute | solution.py:31
  36.0 32.5 %collective-permute-start.2 = (f32[8,256]{1,0:T(8,128)S(1)}, f32[8,256]{1,0:T(8,128)S(1)}, u32[]{:S(2)}, u32[]{:S(2)}) collective-permute-start(f32[8,256]{1,0:T(8,128)S(1)} %reduce_sum.27), channel_id=1, source_target_pairs={{0,8},{1,9},{2,10},{3,11},{4,12},{5,13},{6,14},{7,15},{8,0},{9,1},... | collective-permute-start | bytes 24584 | tf_op jit(solution)/shard_map/ppermute | solution.py:31
  68.5 5.8 %collective-permute-start.7 = (f32[8,256]{1,0:T(8,128)S(1)}, f32[8,256]{1,0:T(8,128)S(1)}, u32[]{:S(2)}, u32[]{:S(2)}) collective-permute-start(f32[8,256]{1,0:T(8,128)S(1)} %add.22.own_sum), channel_id=1, source_target_pairs={{64,192},{65,193},{66,194},{67,195},{68,196},{69,197},{70,198},{71... | collective-permute-start | bytes 24584 | tf_op jit(solution)/shard_map/ppermute | solution.py:31
  70.4 9.5 %collective-permute-start.1 = (f32[16,256]{1,0:T(8,128)S(1)}, f32[16,256]{1,0:T(8,128)S(1)}, u32[]{:S(2)}, u32[]{:S(2)}) collective-permute-start(f32[16,256]{1,0:T(8,128)S(1)} %get-tuple-element.16), channel_id=1, source_target_pairs={{0,127},{1,64},{2,65},{3,66},{4,67},{5,68},{6,69},{7,70},{8,71},{9... | collective-permute-start | bytes 49160 | tf_op jit(solution)/shard_map/ppermute | solution.py:31
  72.4 9.5 %collective-permute-start.3 = (f32[8,256]{1,0:T(8,128)S(1)}, f32[8,256]{1,0:T(8,128)S(1)}, u32[]{:S(2)}, u32[]{:S(2)}) collective-permute-start(f32[8,256]{1,0:T(8,128)S(1)} %add.22.own_sum), channel_id=1, source_target_pairs={{0,72},{1,73},{2,74},{3,75},{4,76},{5,77},{6,78},{7,79},{8,64},{9,... | collective-permute-start | bytes 24584 | tf_op jit(solution)/shard_map/ppermute | solution.py:31
  74.4 1.4 copy-start.5
  83.6 6.9 %collective-permute-start.8 = (f32[32,16,256]{2,1,0:T(8,128)S(1)}, f32[32,16,256]{2,1,0:T(8,128)S(1)}, u32[]{:S(2)}, u32[]{:S(2)}) collective-permute-start(f32[32,16,256]{2,1,0:T(8,128)S(1)} %get-tuple-element.24), channel_id=1, source_target_pairs={{0,1},{1,0},{2,3},{3,2},{4,5},{5,4},{6,7},{7,6},{8,9},{9,8},{10,11... | collective-permute-start | bytes 1572872 | tf_op jit(solution)/shard_map/ppermute | solution.py:31
  105.4 13.7 %all-to-all-start.2 = ((f32[4,2,16,256]{3,2,1,0:T(8,128)}), f32[4,2,16,256]{3,2,1,0:T(8,128)S(1)}, u32[]{:S(2)}, u32[]{:S(2)}) async-start(f32[4,2,16,256]{3,2,1,0:T(8,128)} %copy.9), calls=%async_computation.2 | async-start | bytes 262144 | tf_op jit(solution)/shard_map/all_to_all | solution.py:45
  119.2 9.5 %collective-permute-start.9 = (f32[16,256]{1,0:T(8,128)S(1)}, f32[16,256]{1,0:T(8,128)S(1)}, u32[]{:S(2)}, u32[]{:S(2)}) collective-permute-start(f32[16,256]{1,0:T(8,128)S(1)} %pad_maximum_fusion), channel_id=1, source_target_pairs={{0,8},{1,9},{2,10},{3,11},{4,12},{5,13},{6,14},{7,15},{8,0},{9,1},... | collective-permute-start | bytes 49160 | tf_op jit(solution)/shard_map/ppermute | solution.py:31
  128.7 5.8 %collective-permute-start.10 = (f32[8,256]{1,0:T(8,128)S(1)}, f32[8,256]{1,0:T(8,128)S(1)}, u32[]{:S(2)}, u32[]{:S(2)}) collective-permute-start(f32[8,256]{1,0:T(8,128)S(1)} %get-tuple-element.29), channel_id=1, source_target_pairs={{0,128},{1,129},{2,130},{3,131},{4,132},{5,133},{6,134},{7,135},{8... | collective-permute-start | bytes 24584 | tf_op jit(solution)/shard_map/ppermute | solution.py:31
  132.3 9.5 %collective-permute-start.11 = (f32[8,256]{1,0:T(8,128)S(1)}, f32[8,256]{1,0:T(8,128)S(1)}, u32[]{:S(2)}, u32[]{:S(2)}) collective-permute-start(f32[8,256]{1,0:T(8,128)S(1)} %get-tuple-element.30), channel_id=1, source_target_pairs={{0,72},{1,73},{2,74},{3,75},{4,76},{5,77},{6,78},{7,79},{8,64},{9,... | collective-permute-start | bytes 24584 | tf_op jit(solution)/shard_map/ppermute | solution.py:31

commit v3 on v2

--- a/solution.py
+++ b/solution.py
@@ -23,8 +23,8 @@
 
 
 def basis_step(x, z, core, by):
-    index = (x * 16 + z * 2 + core + by) % 64
-    return index // 16, index // 2 % 8, index % 2
+    index = x * 16 + z * 2 + core + by
+    return (index // 16, index // 2 % 8, index % 2) if 0 <= index < 64 else None
 
 
 def move(array, target):
@@ -35,53 +35,44 @@
     return [x * 16 + z * 2 + core for x in xs for z in zs for core in cores]
 
 
-quarters = (range(4), range(4, 8))
 x_groups = [ring(range(4), (z,), (core,)) for z in range(8) for core in range(2)]
-z_groups = [ring((x,), q, (core,)) for x in range(4) for q in quarters for core in range(2)]
-cube_groups = [ring(range(4), q, range(2)) for q in quarters]
+z_groups = [ring((x,), range(8), (core,)) for x in range(4) for core in range(2)]
+plane_groups = [ring(range(4), (z,), range(2)) for z in range(8)]
 
 
 def spread(array, groups):
     return lax.all_to_all(array, "basis", 0, 0, axis_index_groups=groups)
 
 
+def gather_sum(array, groups):
+    count = len(groups[0])
+    return spread(jnp.broadcast_to(array[None], (count, *array.shape)), groups).sum(0)
+
+
 def swap_core(y, h, x, z, core):
     return y, h, x, z, 1 - core
 
 
-def swap_quarter(y, h, x, z, core):
-    return y, h, x, z ^ 4, core
-
-
 def swap_parity(y, h, x, z, core):
     return y, 1 - h, x, z, core
 
 
-def swap_both(y, h, x, z, core):
-    return y, 1 - h, x, z ^ 4, core
-
-
 def to_neighbour(y, h, x, z, core):
-    to = y - 1 if h == 0 else y + 1
-    return (to, h, x, z, core) if 0 <= to < 4 else None
+    return ((y - 1) if h == 0 else (y + 1)) % 4, h, x, z, core
 
 
 def from_neighbour(y, h, x, z, core):
-    to = y + 1 if h == 0 else y - 1
-    return (to, h, x, z, core) if 0 <= to < 4 else None
+    return ((y + 1) if h == 0 else (y - 1)) % 4, h, x, z, core
 
 
 def halo_own(y, h, x, z, core):
-    return (y, h, *basis_step(x, z, core, 1 if h == 0 else -1))
+    to = basis_step(x, z, core, 1 if h == 0 else -1)
+    return None if to is None else (y, h, *to)
 
 
 def halo_visitor(y, h, x, z, core):
-    return (y, 1 - h, *basis_step(x, z, core, -1 if h == 0 else 1))
-
-
-def halo_neighbour(y, h, x, z, core):
-    to = y - 1 if h == 0 else y + 1
-    return (to, h, *basis_step(x, z, core, 1 if h == 0 else -1)) if 0 <= to < 4 else None
+    to = basis_step(x, z, core, -1 if h == 0 else 1)
+    return None if to is None else (y, 1 - h, *to)
 
 
 def product(a, b):
@@ -115,7 +106,7 @@
     out_picked[...] = jnp.broadcast_to(picked[None], out_picked.shape)
     even = h == 0
     depth = lax.broadcasted_iota(jnp.int32, band.shape, 0) + 1
-    masked = jnp.where(depth <= reach[...], band[...], 0.0)
+    masked = jnp.where(depth <= reach[...].reshape(1, rows), band[...], 0.0)
     out_rim[0:edge, :] = jnp.where(even, own[rows - edge :, :], own[:edge, :])
     out_rim[edge : 2 * edge, :] = jnp.zeros((edge, width), jnp.float32)
     out_rim[edge : edge + band.shape[0], :] = masked[:, rows - width :]
@@ -124,7 +115,7 @@
     out_visitor[edge:, :] = ends_last[0]
 
 
-def apply(own, near, ends, own_rim, near_rim, own_sum, near_sum, diag, band, reach,
+def apply(own, near, ends, own_rim, near_rim, own_sum, diag, band, reach,
           out_slope, out_own, out_near, out_curve, own_f, near_f, slope_f, weight_f, turned, applied_f, own_w, near_w, slope_w, weight_w):
     y, h, basis = place()
     rows, width = own.shape
@@ -135,7 +126,7 @@
     at_far = (even & (y == 3)) | ((h == 1) & (y == 0))
     far = 1 - h
     own_sign = sign_of(own_sum[0:1, :])
-    near_sign = sign_of(near_sum[0:1, :])
+    near_sign = sign_of(near_rim[edge : edge + 1, :])
     has_low = (even & (basis > 0)).astype(jnp.float32)
     has_high = ((h == 1) & (basis < 63)).astype(jnp.float32)
     blank = jnp.zeros((pad, width), jnp.float32)
@@ -152,14 +143,15 @@
         near_f[edge:pad, :] = own_rim[2 * edge :, :] * has_low
         near_f[pad + rows : pad + rows + edge, :] = own_rim[2 * edge :, :] * has_high
 
-    @pl.when(jnp.logical_not(at_far))
-    def _():
+    def fill_near():
         near_f[pad : pad + rows, :] = near[...] * near_sign
         near_f[edge:pad, :] = near_rim[0:edge, :] * near_sign * has_low
         near_f[pad + rows : pad + rows + edge, :] = near_rim[0:edge, :] * near_sign * has_high
 
+    pl.when(jnp.logical_not(at_far))(fill_near)
     turn = jnp.where(even, 1.0, -1.0)
     slope_f[...] = (near_f[...] - own_f[...]) * turn / (2.0 * radial_step)
+    pl.when(at_far)(fill_near)
 
     count = band.shape[0]
     depth = lax.broadcasted_iota(jnp.int32, band.shape, 0) + 1
@@ -208,7 +200,7 @@
             out[start : start + step, :] = jnp.where(inside, banded(held, weight_w, start + edge, step), 0.0)
 
 
-def multiply(visitor, visitor_rim, visitor_sum, ends, slope_applied, own_applied, near_applied, curve,
+def multiply(visitor, visitor_rim, ends, slope_applied, own_applied, near_applied, curve,
              out_keep, out_send, seen, moved):
     y, h, basis = place()
     even = h == 0
@@ -216,24 +208,22 @@
     rows = ends.shape[1]
     half = rows // 2
     size = half + edge
-    at_near = (even & (y == 0)) | ((h == 1) & (y == 3))
+    at_far = (even & (y == 3)) | ((h == 1) & (y == 0))
     at = pl.multiple_of(jnp.where(even, edge, 0), edge)
-    visitor_sign = sign_of(visitor_sum[0:1, :])
-    seen[0:edge, :] = visitor_rim[0:edge, :] * visitor_sign
-    seen[size:, :] = visitor_rim[0:edge, :] * visitor_sign
-    seen[pl.ds(at, size), :] = visitor[...] * visitor_sign
+    seen[0:edge, :] = visitor_rim[0:edge, :]
+    seen[size:, :] = visitor_rim[0:edge, :]
+    seen[pl.ds(at, size), :] = visitor[...]
     moved[...] = seen[...]
 
-    @pl.when(at_near)
+    @pl.when(at_far)
     def _():
-        moved[0:edge, :] = moved[0:edge, :] - visitor_rim[edge : 2 * edge, :]
-        beside = ends[h, pl.ds(pl.multiple_of(h * (half - edge), edge), size), :]
-        moved[pl.ds(at, size), :] = seen[pl.ds(at, size), :] - beside
+        moved[0:edge, :] = visitor_rim[edge : 2 * edge, :]
+        moved[pl.ds(at, size), :] = ends[h, pl.ds(pl.multiple_of(h * (half - edge), edge), size), :]
 
     scale = 1.0 / (2.0 * radial_step)
     cross = product(seen[...], slope_applied[...])
-    first = product(own_applied[...], moved[...] * scale)
-    second = product(near_applied[...], seen[...] * scale)
+    first = product(own_applied[...], seen[...] * scale)
+    second = product(near_applied[...], moved[...] * scale)
     low = core == 0
     for index, part in enumerate((cross, curve[...], first, second)):
         part = part.reshape(32, 2 * 4, part.shape[1])
@@ -242,47 +232,56 @@
         out_send[:, 4 * index : 4 * index + 4, :] = jnp.where(low, back, front)
 
 
-def kernel(body, shapes, scratch, work, *operands, in_specs=None):
-    extra = {} if in_specs is None else {"in_specs": in_specs}
+def kernel(body, shapes, scratch, work, *operands):
     return pl.pallas_call(
         body,
         out_shape=[jax.ShapeDtypeStruct(shape, jnp.float32) for shape in shapes],
         scratch_shapes=[pltpu.VMEM(shape, jnp.float32) for shape in scratch],
         compiler_params=pltpu.CompilerParams(vmem_limit_bytes=40 * 1024 * 1024),
         cost_estimate=pl.CostEstimate(flops=work, bytes_accessed=4 * 1024 * 1024, transcendentals=0),
-        **extra,
     )(*operands)
+
+
+def whole(shape):
+    return pl.BlockSpec(shape, lambda i: (0,) * len(shape))
 
 
 def shards(panels, end_panels, correlation_diag, correlation_band, band_reach, sign_rows):
     own = panels[0]
     rows, width = own.shape
     half = rows // 2
-    rho, basis = lax.axis_index("rho"), lax.axis_index("basis")
-    h, quarter = rho % 2, basis // 8 % 2
+    h = lax.axis_index("rho") % 2
     reach = band_reach[None, :]
 
-    half_rows, rim, visitor_rim, picked = kernel(
+    half_rows, rim, visitor_rim, picked = pl.pallas_call(
         prepare,
-        [(half + edge, width), (3 * edge, width), (2 * edge, width), (32, edge, width)],
-        [],
-        1000000,
-        own,
-        end_panels[:, :edge],
-        end_panels[:, rows - edge :],
-        correlation_band,
-        reach,
-        sign_rows,
+        grid=(1,),
+        in_specs=[
+            whole(own.shape),
+            whole((2, edge, width)),
+            pl.BlockSpec((2, edge, width), lambda i: (0, rows // edge - 1, 0)),
+            whole(correlation_band.shape),
+            whole(band_reach.shape),
+            whole(sign_rows.shape),
+        ],
+        out_specs=[whole((half + edge, width)), whole((3 * edge, width)), whole((2 * edge, width)), whole((8, edge, width))],
+        out_shape=[
+            jax.ShapeDtypeStruct(shape, jnp.float32)
+            for shape in ((half + edge, width), (3 * edge, width), (2 * edge, width), (8, edge, width))
+        ],
+        compiler_params=pltpu.CompilerParams(vmem_limit_bytes=60 * 1024 * 1024),
+        cost_estimate=pl.CostEstimate(flops=1000000, bytes_accessed=2 * 1024 * 1024, transcendentals=0),
+    )(own, end_panels, end_panels, correlation_band, band_reach, sign_rows)
+    own_rim = move(rim, halo_own)
+    picked = spread(picked, z_groups).sum(0)
+    half_rows, picked, own_rim, visitor_rim, own = lax.optimization_barrier(
+        (half_rows, picked, own_rim, visitor_rim, own)
     )
     visitor = move(half_rows, swap_parity)
-    picked = spread(picked, cube_groups).sum(0)
+    visitor_rim = move(visitor_rim, halo_visitor)
     near = move(own, to_neighbour)
-    own_rim = move(rim, halo_own)
-    near_rim = move(rim, halo_neighbour)
-    visitor_rim = move(visitor_rim, halo_visitor)
-    own_sum = picked + move(picked, swap_quarter)
-    near_sum = move(own_sum, to_neighbour)
-    visitor_sum = move(own_sum, swap_both)
+    own_sum = gather_sum(picked, plane_groups)
+    near_rim = move(jnp.concatenate([own_rim[:edge], own_sum]), to_neighbour)
 
     window = half + 4 * edge
     frame = rows + 4 * edge
@@ -294,28 +293,28 @@
         + [(window, width)] * 3
         + [(window, 2 * edge)],
         1000000000,
-        own, near, end_panels, own_rim, near_rim, own_sum, near_sum, correlation_diag[None, :], correlation_band, reach,
+        own, near, end_panels, own_rim, near_rim, own_sum, correlation_diag[None, :], correlation_band, reach,
     )
     keep, send = kernel(
         multiply,
         [(32, 16, width)] * 2,
         [(half + 2 * edge, width)] * 2,
         1000000000,
-        visitor, visitor_rim, visitor_sum, end_panels, slope_applied, own_applied, near_applied, curve,
+        visitor, visitor_rim, end_panels, slope_applied, own_applied, near_applied, curve,
     )
     mine = keep + move(send, swap_core)
     mine = spread(mine.reshape(4, 8, 16, width), x_groups).sum(0)
-    mine = spread(mine.reshape(2, 4, 16, width).transpose(1, 0, 2, 3), z_groups).sum(0)
-    here = quarter == 0
-    low, high = mine[0], mine[1]
-    stay = jnp.where(here, low, high)
-    go = jnp.where(here, high, low)
-    mine = jnp.concatenate([go[:8], stay[8:]]) + move(jnp.concatenate([stay[:8], go[8:]]), swap_quarter)
-    away = move(mine[:8], swap_both)
+    mine = spread(mine, z_groups).sum(0)
+    y, basis = lax.axis_index("rho") // 2, lax.axis_index("basis")
+    at_far = jnp.where(h == 0, y == 3, y == 0)
+    line = jnp.arange(edge)[:, None]
+    signs = jnp.where(line == 0, jnp.sign(own_sum), jnp.where(at_far, 1.0, jnp.sign(near_rim[edge:])))
+    away = move(jnp.concatenate([mine[:8], signs]), swap_parity)
     second = move(mine[8:], from_neighbour)[4:]
     turn = jnp.where(h == 0, 1.0, -1.0)
-    drift = turn * (mine[8:12] - second) + away[:4]
-    return jnp.stack([drift, away[4:]], axis=1)[:, None]
+    here = lax.dynamic_slice_in_dim(signs[0], basis * 4, 4)[:, None]
+    drift = turn * (mine[8:12] * away[8] - second * away[9]) + here * away[:4]
+    return jnp.stack([drift, away[4:8]], axis=1)[:, None]
 
 
 def solution(mesh):

time: 143 us -> 132 us (0.923)
  waiting for transfers between devices: 51.4 us -> 40.8 us
  local copies, waits for them, and re-layouts: 6.07 us -> 1.35 us
  Pallas kernels: 6.74 us -> 9.09 us
    ppermute x12 -> x8, waiting for transfers between devices: 45.5 us -> 14.3 us  [move(): return lax.ppermute(array, both, hops(target))]
    all_to_all x2 -> x3, waiting for transfers between devices: 5.92 us -> 26.4 us  [spread(): return lax.all_to_all(array, 'basis', 0, 0, axis_index_groups=groups)]
    all_to_all x2 -> x3, starting transfers between devices: 16.5 us -> 29.5 us  [spread(): return lax.all_to_all(array, 'basis', 0, 0, axis_index_groups=groups)]
    ppermute x12 -> x8, starting transfers between devices: 46.5 us -> 34 us  [move(): return lax.ppermute(array, both, hops(target))]
    unnamed x14 -> x10, local copies, waits for them, and re-layouts: 3.93 us -> 0.02 us
    pallas_call x0 -> x1, Pallas kernels: none -> 2.17 us  [shards(): pl.pallas_call(prepare, grid=(1,), in_specs=[whole(own.shape), whole((2,...]
    pallas_call x3 -> x2, Pallas kernels: 6.74 us -> 6.92 us  [kernel(): pl.pallas_call(body, out_shape=[jax.ShapeDtypeStruct(shape, jnp.float32)...]
  transfers between devices with their start and end apart: 14 -> 11, of which waited for: 6 -> 7; matrix products, arithmetic and copies ran while one was open for 0% -> 1% of each run, Pallas kernels for 3% -> 3%
where the time goes in v3:
time: 132 us; the launch traced here: 131 us
  starting transfers between devices  63.5 us (48%)
  waiting for transfers between devices  40.8 us (31%)
  blocking collectives  15.1 us (11%)
  Pallas kernels  9.09 us (7%)
  local copies, waits for them, and re-layouts  1.35 us (1%)
    ppermute x8, starting transfers between devices, move(): return lax.ppermute(array, both, hops(target))  34 us
    all_to_all x3, starting transfers between devices, spread(): return lax.all_to_all(array, 'basis', 0, 0, axis_index_groups=groups)  29.5 us
    all_to_all x3, waiting for transfers between devices, spread(): return lax.all_to_all(array, 'basis', 0, 0, axis_index_groups=groups)  26.4 us
    all_to_all x1, blocking collectives, spread(): return lax.all_to_all(array, 'basis', 0, 0, axis_index_groups=groups)  15.1 us
    ppermute x8, waiting for transfers between devices, move(): return lax.ppermute(array, both, hops(target))  14.3 us
    pallas_call x2, Pallas kernels, kernel(): pl.pallas_call(body, out_shape=[jax.ShapeDtypeStruct(shape, jnp.float32)...  6.92 us
  transfers between devices with their start and end apart: 11, of which 7 were waited for; matrix products, arithmetic and copies ran while one was open for 1% of the time, Pallas kernels for 3%

profile of v3, /device:TPU:8, one launch (start us, length us, event | category | flops | bytes accessed | tf_op | source)
XLA Modules:
  0.0 131.0 jit_solution(6531144465251892689)
XLA Ops:
  0.0 2.2 %shard_map.64 = (f32[392,256]{1,0:T(8,128)}, f32[24,256]{1,0:T(8,128)}, f32[16,256]{1,0:T(8,128)}, f32[8,8,256]{2,1,0:T(8,128)}) custom-call(f32[768,256]{1,0:T(8,128)} %bitcast.12, f32[2,768,256]{2,1,0:T(8,128)} %ends.3, f32[2,768,256]{2,1,0:T(8,128)} %ends.3, f32[3,768]{1,0:T(4,128)} %band.3, s32[768]{0:T(1024)} %reach.1, s32[1,256]{1,0:T(1,128)} %rows_of.1), custom_call_target="tpu_custom_call" | custom-call | flops 1000000 | bytes 2097152 | tf_op jit(solution)/shard_map/pallas_call | solution.py:256
  2.2 12.5 %all-to-all-start = ((f32[8,8,256]{2,1,0:T(8,128)}), f32[8,8,256]{2,1,0:T(8,128)S(1)}, u32[]{:S(2)}, u32[]{:S(2)}) async-start(f32[8,8,256]{2,1,0:T(8,128)} %get-tuple-element.21), calls=%async_computation | async-start | bytes 131072 | tf_op jit(solution)/shard_map/all_to_all | solution.py:44
  14.7 1.4 %collective-permute-start = (f32[24,256]{1,0:T(8,128)}, f32[24,256]{1,0:T(8,128)S(1)}, u32[]{:S(2)}, u32[]{:S(2)}) collective-permute-start(f32[24,256]{1,0:T(8,128)} %get-tuple-element.22), channel_id=1, source_target_pairs={{0,1},{1,2},{2,3},{3,4},{4,5},{5,6},{6,7},{7,8},{8,9},{9,10},{10,1... | collective-permute-start | bytes 73736 | tf_op jit(solution)/shard_map/ppermute | solution.py:31
  16.2 9.4 %all-to-all-done = f32[8,8,256]{2,1,0:T(8,128)S(1)} async-done(((f32[8,8,256]{2,1,0:T(8,128)}), f32[8,8,256]{2,1,0:T(8,128)S(1)}, u32[]{:S(2)}, u32[]{:S(2)}) %all-to-all-start) | async-done | bytes 65568 | tf_op jit(solution)/shard_map/all_to_all | solution.py:44
  25.7 2.4 %collective-permute-start.3 = (f32[768,256]{1,0:T(8,128)S(1)}, f32[768,256]{1,0:T(8,128)S(1)}, u32[]{:S(2)}, u32[]{:S(2)}) collective-permute-start(f32[768,256]{1,0:T(8,128)S(1)} %bitcast.13), channel_id=1, source_target_pairs={{0,384},{1,385},{2,386},{3,387},{4,388},{5,389},{6,390},{7,391},{8... | collective-permute-start | bytes 2359304 | tf_op jit(solution)/shard_map/ppermute | solution.py:31
  28.0 9.4 %collective-permute-start.1 = (f32[392,256]{1,0:T(8,128)}, f32[392,256]{1,0:T(8,128)}, u32[]{:S(2)}, u32[]{:S(2)}) collective-permute-start(f32[392,256]{1,0:T(8,128)} %get-tuple-element.24), channel_id=1, source_target_pairs={{0,64},{1,65},{2,66},{3,67},{4,68},{5,69},{6,70},{7,71},{8,72},{9,... | collective-permute-start | bytes 1204232 | tf_op jit(solution)/shard_map/ppermute | solution.py:31
  37.4 0.6 broadcast_in_dim.29
  38.0 4.5 %all-to-all-start.1 = ((f32[8,8,256]{2,1,0:T(8,128)}), f32[8,8,256]{2,1,0:T(8,128)S(1)}, u32[]{:S(2)}, u32[]{:S(2)}) async-start(f32[8,8,256]{2,1,0:T(8,128)} %broadcast_in_dim.29), calls=%async_computation.1 | async-start | bytes 131072 | tf_op jit(solution)/shard_map/all_to_all | solution.py:44
  42.5 5.6 %all-to-all-done.1 = f32[8,8,256]{2,1,0:T(8,128)S(1)} async-done(((f32[8,8,256]{2,1,0:T(8,128)}), f32[8,8,256]{2,1,0:T(8,128)S(1)}, u32[]{:S(2)}, u32[]{:S(2)}) %all-to-all-start.1) | async-done | bytes 65568 | tf_op jit(solution)/shard_map/all_to_all | solution.py:44
  48.1 2.4 %collective-permute-start.4 = (f32[16,256]{1,0:T(8,128)S(1)}, f32[16,256]{1,0:T(8,128)S(1)}, u32[]{:S(2)}, u32[]{:S(2)}) collective-permute-start(f32[16,256]{1,0:T(8,128)S(1)} %pad_maximum_fusion), channel_id=1, source_target_pairs={{0,384},{1,385},{2,386},{3,387},{4,388},{5,389},{6,390},{7,391},{8... | collective-permute-start | bytes 49160 | tf_op jit(solution)/shard_map/ppermute | solution.py:31
  50.5 0.7 collective-permute-start.2
  51.2 2.6 %collective-permute-done.4.near_rim = f32[16,256]{1,0:T(8,128)S(1)} collective-permute-done((f32[16,256]{1,0:T(8,128)S(1)}, f32[16,256]{1,0:T(8,128)S(1)}, u32[]{:S(2)}, u32[]{:S(2)}) %collective-permute-start.4) | collective-permute-done | bytes 16416 | tf_op jit(solution)/shard_map/ppermute | solution.py:31
  53.8 4.2 %shard_map.65 = (f32[400,256]{1,0:T(8,128)S(1)}, f32[400,256]{1,0:T(8,128)S(1)}, f32[400,256]{1,0:T(8,128)S(1)}, f32[256,256]{1,0:T(8,128)S(1)}) custom-call(f32[768,256]{1,0:T(8,128)S(1)} %bitcast.14, f32[768,256]{1,0:T(8,128)S(1)} %collective-permute-done.3.near, f32[2,768,256]{2,1,0:T(8,128)S(1)} %copy-done, f32[24,256]{1,0:T(8,128)S(1)} %collective-permute-done.own_rim, ...), custom_call_target="tpu_custom_call" | custom-call | flops 1000000000 | bytes 4194304 | tf_op jit(solution)/shard_map/pallas_call | solution.py:236
  58.0 5.7 %collective-permute-done.1.visitor = f32[392,256]{1,0:T(8,128)} collective-permute-done((f32[392,256]{1,0:T(8,128)}, f32[392,256]{1,0:T(8,128)}, u32[]{:S(2)}, u32[]{:S(2)}) %collective-permute-start.1) | collective-permute-done | bytes 401440 | tf_op jit(solution)/shard_map/ppermute | solution.py:31
  63.7 2.7 %shard_map.66 = (f32[32,16,256]{2,1,0:T(8,128)S(1)}, f32[32,16,256]{2,1,0:T(8,128)S(1)}) custom-call(f32[392,256]{1,0:T(8,128)} %collective-permute-done.1.visitor, f32[16,256]{1,0:T(8,128)S(1)} %collective-permute-done.2.visitor_rim, f32[2,768,256]{2,1,0:T(8,128)S(1)} %copy-done, f32[400,256]{1,0:T(8,128)S(1)} %get-tuple-element.29.slope_applied, ...), custom_call_target="tpu_custom_call" | custom-call | flops 1000000000 | bytes 4194304 | tf_op jit(solution)/shard_map/pallas_call | solution.py:236
  66.4 8.1 %collective-permute-start.5 = (f32[32,16,256]{2,1,0:T(8,128)S(1)}, f32[32,16,256]{2,1,0:T(8,128)S(1)}, u32[]{:S(2)}, u32[]{:S(2)}) collective-permute-start(f32[32,16,256]{2,1,0:T(8,128)S(1)} %get-tuple-element.34), channel_id=1, source_target_pairs={{0,1},{1,0},{2,3},{3,2},{4,5},{5,4},{6,7},{7,6},{8,9},{9,8},{10,11... | collective-permute-start | bytes 1572872 | tf_op jit(solution)/shard_map/ppermute | solution.py:31
  74.5 1.5 %collective-permute-done.5 = f32[32,16,256]{2,1,0:T(8,128)S(1)} collective-permute-done((f32[32,16,256]{2,1,0:T(8,128)S(1)}, f32[32,16,256]{2,1,0:T(8,128)S(1)}, u32[]{:S(2)}, u32[]{:S(2)}) %collective-permute-start.5) | collective-permute-done | bytes 524320 | tf_op jit(solution)/shard_map/ppermute | solution.py:31
  76.1 15.1 %all_to_all.20 = f32[4,8,16,256]{3,2,1,0:T(8,128)S(1)} all-to-all(f32[4,8,16,256]{3,2,1,0:T(8,128)S(1)} %bitcast.15), channel_id=1, replica_groups={{0,16,32,48},{1,17,33,49},{2,18,34,50},{3,19,35,51},{4,20,36,52},{5,21,..., dimensions={0} | all-to-all | bytes 1048576 | tf_op jit(solution)/shard_map/all_to_all | solution.py:44
  91.3 0.7 reduce_sum.38
  91.9 12.5 %all-to-all-start.3 = ((f32[8,16,256]{2,1,0:T(8,128)}), f32[8,16,256]{2,1,0:T(8,128)S(1)}, u32[]{:S(2)}, u32[]{:S(2)}) async-start(f32[8,16,256]{2,1,0:T(8,128)} %reduce_sum.38), calls=%async_computation.3 | async-start | bytes 262144 | tf_op jit(solution)/shard_map/all_to_all | solution.py:44
  104.6 11.4 %all-to-all-done.3 = f32[8,16,256]{2,1,0:T(8,128)S(1)} async-done(((f32[8,16,256]{2,1,0:T(8,128)}), f32[8,16,256]{2,1,0:T(8,128)S(1)}, u32[]{:S(2)}, u32[]{:S(2)}) %all-to-all-start.3) | async-done | bytes 131104 | tf_op jit(solution)/shard_map/all_to_all | solution.py:44
  116.0 6.4 %collective-permute-start.6 = (f32[16,256]{1,0:T(8,128)S(1)}, f32[16,256]{1,0:T(8,128)S(1)}, u32[]{:S(2)}, u32[]{:S(2)}) collective-permute-start(f32[16,256]{1,0:T(8,128)S(1)} %pad_maximum_fusion.1), channel_id=1, source_target_pairs={{0,64},{1,65},{2,66},{3,67},{4,68},{5,69},{6,70},{7,71},{8,72},{9,... | collective-permute-start | bytes 49160 | tf_op jit(solution)/shard_map/ppermute | solution.py:31
  122.5 3.3 %collective-permute-start.7 = (f32[8,256]{1,0:T(8,128)S(1)}, f32[8,256]{1,0:T(8,128)S(1)}, u32[]{:S(2)}, u32[]{:S(2)}) collective-permute-start(f32[8,256]{1,0:T(8,128)S(1)} %get-tuple-element.39), channel_id=1, source_target_pairs={{0,128},{1,129},{2,130},{3,131},{4,132},{5,133},{6,134},{7,135},{8... | collective-permute-start | bytes 24584 | tf_op jit(solution)/shard_map/ppermute | solution.py:31
  125.7 4.6 %collective-permute-done.6 = f32[16,256]{1,0:T(8,128)S(1)} collective-permute-done((f32[16,256]{1,0:T(8,128)S(1)}, f32[16,256]{1,0:T(8,128)S(1)}, u32[]{:S(2)}, u32[]{:S(2)}) %collective-permute-start.6) | collective-permute-done | bytes 16416 | tf_op jit(solution)/shard_map/ppermute | solution.py:31
  (32 shorter events, 1.0 us)
Async XLA Ops:
  0.0 25.7 %copy-start.1 = (f32[1,768,256]{2,1,0:T(8,128)S(1)}, f32[1,768,256]{2,1,0:T(8,128)}, u32[]{:S(2)}) copy-start(f32[1,768,256]{2,1,0:T(8,128)} %param.6) | copy-start | bytes 2359300
  0.0 50.5 %copy-start.3 = (s32[768]{0:T(1024)S(1)}, s32[768]{0:T(1024)}, u32[]{:S(2)}) copy-start(s32[768]{0:T(1024)} %reach.1) | copy-start | bytes 9220
  0.0 50.5 %copy-start.4 = (f32[768]{0:T(1024)S(1)}, f32[768]{0:T(1024)}, u32[]{:S(2)}) copy-start(f32[768]{0:T(1024)} %param.8) | copy-start | bytes 9220
  0.0 53.8 %copy-start = (f32[2,768,256]{2,1,0:T(8,128)S(1)}, f32[2,768,256]{2,1,0:T(8,128)}, u32[]{:S(2)}) copy-start(f32[2,768,256]{2,1,0:T(8,128)} %ends.3) | copy-start | bytes 4718596
  0.0 53.7 %copy-start.2 = (f32[3,768]{1,0:T(4,128)S(1)}, f32[3,768]{1,0:T(4,128)}, u32[]{:S(2)}) copy-start(f32[3,768]{1,0:T(4,128)} %band.3) | copy-start | bytes 27652
  2.2 23.4 %all-to-all-start = ((f32[8,8,256]{2,1,0:T(8,128)}), f32[8,8,256]{2,1,0:T(8,128)S(1)}, u32[]{:S(2)}, u32[]{:S(2)}) async-start(f32[8,8,256]{2,1,0:T(8,128)} %get-tuple-element.21), calls=%async_computation | async-start | bytes 131072 | tf_op jit(solution)/shard_map/all_to_all | solution.py:44
  14.7 10.9 %collective-permute-start = (f32[24,256]{1,0:T(8,128)}, f32[24,256]{1,0:T(8,128)S(1)}, u32[]{:S(2)}, u32[]{:S(2)}) collective-permute-start(f32[24,256]{1,0:T(8,128)} %get-tuple-element.22), channel_id=1, source_target_pairs={{0,1},{1,2},{2,3},{3,4},{4,5},{5,6},{6,7},{7,8},{8,9},{9,10},{10,1... | collective-permute-start | bytes 73736 | tf_op jit(solution)/shard_map/ppermute | solution.py:31
  25.7 28.1 %collective-permute-start.3 = (f32[768,256]{1,0:T(8,128)S(1)}, f32[768,256]{1,0:T(8,128)S(1)}, u32[]{:S(2)}, u32[]{:S(2)}) collective-permute-start(f32[768,256]{1,0:T(8,128)S(1)} %bitcast.13), channel_id=1, source_target_pairs={{0,384},{1,385},{2,386},{3,387},{4,388},{5,389},{6,390},{7,391},{8... | collective-permute-start | bytes 2359304 | tf_op jit(solution)/shard_map/ppermute | solution.py:31
  28.0 35.6 %collective-permute-start.1 = (f32[392,256]{1,0:T(8,128)}, f32[392,256]{1,0:T(8,128)}, u32[]{:S(2)}, u32[]{:S(2)}) collective-permute-start(f32[392,256]{1,0:T(8,128)} %get-tuple-element.24), channel_id=1, source_target_pairs={{0,64},{1,65},{2,66},{3,67},{4,68},{5,69},{6,70},{7,71},{8,72},{9,... | collective-permute-start | bytes 1204232 | tf_op jit(solution)/shard_map/ppermute | solution.py:31
  38.0 10.1 %all-to-all-start.1 = ((f32[8,8,256]{2,1,0:T(8,128)}), f32[8,8,256]{2,1,0:T(8,128)S(1)}, u32[]{:S(2)}, u32[]{:S(2)}) async-start(f32[8,8,256]{2,1,0:T(8,128)} %broadcast_in_dim.29), calls=%async_computation.1 | async-start | bytes 131072 | tf_op jit(solution)/shard_map/all_to_all | solution.py:44
  48.1 5.6 %collective-permute-start.4 = (f32[16,256]{1,0:T(8,128)S(1)}, f32[16,256]{1,0:T(8,128)S(1)}, u32[]{:S(2)}, u32[]{:S(2)}) collective-permute-start(f32[16,256]{1,0:T(8,128)S(1)} %pad_maximum_fusion), channel_id=1, source_target_pairs={{0,384},{1,385},{2,386},{3,387},{4,388},{5,389},{6,390},{7,391},{8... | collective-permute-start | bytes 49160 | tf_op jit(solution)/shard_map/ppermute | solution.py:31
  50.5 7.4 %collective-permute-start.2 = (f32[16,256]{1,0:T(8,128)}, f32[16,256]{1,0:T(8,128)S(1)}, u32[]{:S(2)}, u32[]{:S(2)}) collective-permute-start(f32[16,256]{1,0:T(8,128)} %get-tuple-element.25), channel_id=1, source_target_pairs={{1,64},{2,65},{3,66},{4,67},{5,68},{6,69},{7,70},{8,71},{9,72},{10... | collective-permute-start | bytes 49160 | tf_op jit(solution)/shard_map/ppermute | solution.py:31
  66.4 9.6 %collective-permute-start.5 = (f32[32,16,256]{2,1,0:T(8,128)S(1)}, f32[32,16,256]{2,1,0:T(8,128)S(1)}, u32[]{:S(2)}, u32[]{:S(2)}) collective-permute-start(f32[32,16,256]{2,1,0:T(8,128)S(1)} %get-tuple-element.34), channel_id=1, source_target_pairs={{0,1},{1,0},{2,3},{3,2},{4,5},{5,4},{6,7},{7,6},{8,9},{9,8},{10,11... | collective-permute-start | bytes 1572872 | tf_op jit(solution)/shard_map/ppermute | solution.py:31
  91.9 24.0 %all-to-all-start.3 = ((f32[8,16,256]{2,1,0:T(8,128)}), f32[8,16,256]{2,1,0:T(8,128)S(1)}, u32[]{:S(2)}, u32[]{:S(2)}) async-start(f32[8,16,256]{2,1,0:T(8,128)} %reduce_sum.38), calls=%async_computation.3 | async-start | bytes 262144 | tf_op jit(solution)/shard_map/all_to_all | solution.py:44
  116.0 14.3 %collective-permute-start.6 = (f32[16,256]{1,0:T(8,128)S(1)}, f32[16,256]{1,0:T(8,128)S(1)}, u32[]{:S(2)}, u32[]{:S(2)}) collective-permute-start(f32[16,256]{1,0:T(8,128)S(1)} %pad_maximum_fusion.1), channel_id=1, source_target_pairs={{0,64},{1,65},{2,66},{3,67},{4,68},{5,69},{6,70},{7,71},{8,72},{9,... | collective-permute-start | bytes 49160 | tf_op jit(solution)/shard_map/ppermute | solution.py:31
  122.5 7.9 %collective-permute-start.7 = (f32[8,256]{1,0:T(8,128)S(1)}, f32[8,256]{1,0:T(8,128)S(1)}, u32[]{:S(2)}, u32[]{:S(2)}) collective-permute-start(f32[8,256]{1,0:T(8,128)S(1)} %get-tuple-element.39), channel_id=1, source_target_pairs={{0,128},{1,129},{2,130},{3,131},{4,132},{5,133},{6,134},{7,135},{8... | collective-permute-start | bytes 24584 | tf_op jit(solution)/shard_map/ppermute | solution.py:31

commit v4 on v3

--- a/solution.py
+++ b/solution.py
@@ -102,7 +102,7 @@
         line = lax.broadcasted_iota(jnp.int32, (step, width), 0) + start
         hit = jnp.where(line == spot, own[start : start + step, :], 0.0)
         picked = picked + hit.reshape(step // edge, edge, width).sum(0)
-    picked = jnp.broadcast_to(picked.sum(0, keepdims=True), (edge, width))
+    picked = picked.sum(0, keepdims=True)
     out_picked[...] = jnp.broadcast_to(picked[None], out_picked.shape)
     even = h == 0
     depth = lax.broadcasted_iota(jnp.int32, band.shape, 0) + 1
@@ -264,24 +264,22 @@
             whole(band_reach.shape),
             whole(sign_rows.shape),
         ],
-        out_specs=[whole((half + edge, width)), whole((3 * edge, width)), whole((2 * edge, width)), whole((8, edge, width))],
+        out_specs=[whole((half + edge, width)), whole((3 * edge, width)), whole((2 * edge, width)), whole((8, 1, width))],
         out_shape=[
             jax.ShapeDtypeStruct(shape, jnp.float32)
-            for shape in ((half + edge, width), (3 * edge, width), (2 * edge, width), (8, edge, width))
+            for shape in ((half + edge, width), (3 * edge, width), (2 * edge, width), (8, 1, width))
         ],
         compiler_params=pltpu.CompilerParams(vmem_limit_bytes=60 * 1024 * 1024),
         cost_estimate=pl.CostEstimate(flops=1000000, bytes_accessed=2 * 1024 * 1024, transcendentals=0),
     )(own, end_panels, end_panels, correlation_band, band_reach, sign_rows)
     own_rim = move(rim, halo_own)
     picked = spread(picked, z_groups).sum(0)
-    half_rows, picked, own_rim, visitor_rim, own = lax.optimization_barrier(
-        (half_rows, picked, own_rim, visitor_rim, own)
-    )
+    near = move(own, to_neighbour)
+    half_rows, picked, own_rim, visitor_rim = lax.optimization_barrier((half_rows, picked, own_rim, visitor_rim))
     visitor = move(half_rows, swap_parity)
     visitor_rim = move(visitor_rim, halo_visitor)
-    near = move(own, to_neighbour)
     own_sum = gather_sum(picked, plane_groups)
-    near_rim = move(jnp.concatenate([own_rim[:edge], own_sum]), to_neighbour)
+    near_rim = move(jnp.concatenate([own_rim[:edge], jnp.broadcast_to(own_sum, (edge, width))]), to_neighbour)
 
     window = half + 4 * edge
     frame = rows + 4 * edge

time: 132 us -> 131 us (level)
  the two profiles are of different devices: /device:TPU:8 before, /device:TPU:32 now
where the time goes in v4:
time: 131 us; the launch traced here: 130 us
  starting transfers between devices  64.9 us (50%)
  waiting for transfers between devices  39.9 us (30%)
  blocking collectives  14 us (11%)
  Pallas kernels  8.93 us (7%)
  local copies, waits for them, and re-layouts  1.33 us (1%)
    ppermute x8, starting transfers between devices, move(): return lax.ppermute(array, both, hops(target))  37.2 us
    all_to_all x3, starting transfers between devices, spread(): return lax.all_to_all(array, 'basis', 0, 0, axis_index_groups=groups)  27.7 us
    all_to_all x3, waiting for transfers between devices, spread(): return lax.all_to_all(array, 'basis', 0, 0, axis_index_groups=groups)  22.6 us
    ppermute x8, waiting for transfers between devices, move(): return lax.ppermute(array, both, hops(target))  17.3 us
    all_to_all x1, blocking collectives, spread(): return lax.all_to_all(array, 'basis', 0, 0, axis_index_groups=groups)  14 us
    pallas_call x2, Pallas kernels, kernel(): pl.pallas_call(body, out_shape=[jax.ShapeDtypeStruct(shape, jnp.float32)...  6.92 us
  transfers between devices with their start and end apart: 11, of which 6 were waited for; matrix products, arithmetic and copies ran while one was open for 1% of the time, Pallas kernels for 5%

profile of v4, /device:TPU:32, one launch (start us, length us, event | category | flops | bytes accessed | tf_op | source)
XLA Modules:
  0.0 130.3 jit_solution(1359119814553085175)
XLA Ops:
  0.0 5.1 %collective-permute-start.3 = (f32[768,256]{1,0:T(8,128)}, f32[768,256]{1,0:T(8,128)S(1)}, u32[]{:S(2)}, u32[]{:S(2)}) collective-permute-start(f32[768,256]{1,0:T(8,128)} %bitcast.15), channel_id=1, source_target_pairs={{0,384},{1,385},{2,386},{3,387},{4,388},{5,389},{6,390},{7,391},{8... | collective-permute-start | bytes 2359304 | tf_op jit(solution)/shard_map/ppermute | solution.py:31
  5.1 2.0 %shard_map.64 = (f32[392,256]{1,0:T(8,128)}, f32[24,256]{1,0:T(8,128)}, f32[16,256]{1,0:T(8,128)}, f32[8,1,256]{2,1,0:T(1,128)}) custom-call(f32[768,256]{1,0:T(8,128)} %bitcast.16, f32[2,768,256]{2,1,0:T(8,128)} %ends.3, f32[2,768,256]{2,1,0:T(8,128)} %ends.3, f32[3,768]{1,0:T(4,128)} %band.3, s32[768]{0:T(1024)} %reach.1, s32[1,256]{1,0:T(1,128)} %rows_of.1), custom_call_target="tpu_custom_call" | custom-call | flops 1000000 | bytes 2097152 | tf_op jit(solution)/shard_map/pallas_call | solution.py:256
  7.1 12.6 %all-to-all-start = ((f32[8,1,256]{2,1,0:T(1,128)}), f32[8,1,256]{2,1,0:T(1,128)S(1)}, u32[]{:S(2)}, u32[]{:S(2)}) async-start(f32[8,1,256]{2,1,0:T(1,128)} %get-tuple-element.20), calls=%async_computation | async-start | bytes 16384 | tf_op jit(solution)/shard_map/all_to_all | solution.py:44
  19.7 1.9 %collective-permute-start = (f32[24,256]{1,0:T(8,128)}, f32[24,256]{1,0:T(8,128)S(1)}, u32[]{:S(2)}, u32[]{:S(2)}) collective-permute-start(f32[24,256]{1,0:T(8,128)} %get-tuple-element.21), channel_id=1, source_target_pairs={{0,1},{1,2},{2,3},{3,4},{4,5},{5,6},{6,7},{7,8},{8,9},{9,10},{10,1... | collective-permute-start | bytes 73736 | tf_op jit(solution)/shard_map/ppermute | solution.py:31
  21.6 7.0 %all-to-all-done = f32[8,1,256]{2,1,0:T(1,128)S(1)} async-done(((f32[8,1,256]{2,1,0:T(1,128)}), f32[8,1,256]{2,1,0:T(1,128)S(1)}, u32[]{:S(2)}, u32[]{:S(2)}) %all-to-all-start) | async-done | bytes 8224 | tf_op jit(solution)/shard_map/all_to_all | solution.py:44
  28.7 6.8 %collective-permute-start.1 = (f32[392,256]{1,0:T(8,128)}, f32[392,256]{1,0:T(8,128)}, u32[]{:S(2)}, u32[]{:S(2)}) collective-permute-start(f32[392,256]{1,0:T(8,128)} %get-tuple-element.23), channel_id=1, source_target_pairs={{0,64},{1,65},{2,66},{3,67},{4,68},{5,69},{6,70},{7,71},{8,72},{9,... | collective-permute-start | bytes 1204232 | tf_op jit(solution)/shard_map/ppermute | solution.py:31
  35.5 0.6 broadcast_in_dim.45
  36.1 4.3 %all-to-all-start.1 = ((f32[8,1,256]{2,1,0:T(1,128)}), f32[8,1,256]{2,1,0:T(1,128)S(1)}, u32[]{:S(2)}, u32[]{:S(2)}) async-start(f32[8,1,256]{2,1,0:T(1,128)} %broadcast_in_dim.45), calls=%async_computation.1 | async-start | bytes 16384 | tf_op jit(solution)/shard_map/all_to_all | solution.py:44
  40.4 5.3 %all-to-all-done.1 = f32[8,1,256]{2,1,0:T(1,128)S(1)} async-done(((f32[8,1,256]{2,1,0:T(1,128)}), f32[8,1,256]{2,1,0:T(1,128)S(1)}, u32[]{:S(2)}, u32[]{:S(2)}) %all-to-all-start.1) | async-done | bytes 8224 | tf_op jit(solution)/shard_map/all_to_all | solution.py:44
  45.8 3.6 %collective-permute-start.4 = (f32[16,256]{1,0:T(8,128)S(1)}, f32[16,256]{1,0:T(8,128)S(1)}, u32[]{:S(2)}, u32[]{:S(2)}) collective-permute-start(f32[16,256]{1,0:T(8,128)S(1)} %pad_maximum_fusion), channel_id=1, source_target_pairs={{0,384},{1,385},{2,386},{3,387},{4,388},{5,389},{6,390},{7,391},{8... | collective-permute-start | bytes 49160 | tf_op jit(solution)/shard_map/ppermute | solution.py:31
  49.4 8.3 %collective-permute-start.2 = (f32[16,256]{1,0:T(8,128)}, f32[16,256]{1,0:T(8,128)S(1)}, u32[]{:S(2)}, u32[]{:S(2)}) collective-permute-start(f32[16,256]{1,0:T(8,128)} %get-tuple-element.24), channel_id=1, source_target_pairs={{1,64},{2,65},{3,66},{4,67},{5,68},{6,69},{7,70},{8,71},{9,72},{10... | collective-permute-start | bytes 49160 | tf_op jit(solution)/shard_map/ppermute | solution.py:31
  57.8 4.2 %shard_map.65 = (f32[400,256]{1,0:T(8,128)S(1)}, f32[400,256]{1,0:T(8,128)S(1)}, f32[400,256]{1,0:T(8,128)S(1)}, f32[256,256]{1,0:T(8,128)S(1)}) custom-call(f32[768,256]{1,0:T(8,128)S(1)} %bitcast.17, f32[768,256]{1,0:T(8,128)S(1)} %collective-permute-done.3.near, f32[2,768,256]{2,1,0:T(8,128)S(1)} %copy-done, f32[24,256]{1,0:T(8,128)S(1)} %collective-permute-done.own_rim, ...), custom_call_target="tpu_custom_call" | custom-call | flops 1000000000 | bytes 4194304 | tf_op jit(solution)/shard_map/pallas_call | solution.py:236
  62.0 10.6 %collective-permute-done.2.visitor_rim = f32[16,256]{1,0:T(8,128)S(1)} collective-permute-done((f32[16,256]{1,0:T(8,128)}, f32[16,256]{1,0:T(8,128)S(1)}, u32[]{:S(2)}, u32[]{:S(2)}) %collective-permute-start.2) | collective-permute-done | bytes 16416 | tf_op jit(solution)/shard_map/ppermute | solution.py:31
  72.5 2.7 %shard_map.66 = (f32[32,16,256]{2,1,0:T(8,128)S(1)}, f32[32,16,256]{2,1,0:T(8,128)S(1)}) custom-call(f32[392,256]{1,0:T(8,128)} %collective-permute-done.1.visitor, f32[16,256]{1,0:T(8,128)S(1)} %collective-permute-done.2.visitor_rim, f32[2,768,256]{2,1,0:T(8,128)S(1)} %copy-done, f32[400,256]{1,0:T(8,128)S(1)} %get-tuple-element.27.slope_applied, ...), custom_call_target="tpu_custom_call" | custom-call | flops 1000000000 | bytes 4194304 | tf_op jit(solution)/shard_map/pallas_call | solution.py:236
  75.3 1.9 %collective-permute-start.5 = (f32[32,16,256]{2,1,0:T(8,128)S(1)}, f32[32,16,256]{2,1,0:T(8,128)S(1)}, u32[]{:S(2)}, u32[]{:S(2)}) collective-permute-start(f32[32,16,256]{2,1,0:T(8,128)S(1)} %get-tuple-element.32), channel_id=1, source_target_pairs={{0,1},{1,0},{2,3},{3,2},{4,5},{5,4},{6,7},{7,6},{8,9},{9,8},{10,11... | collective-permute-start | bytes 1572872 | tf_op jit(solution)/shard_map/ppermute | solution.py:31
  77.2 1.9 %collective-permute-done.5 = f32[32,16,256]{2,1,0:T(8,128)S(1)} collective-permute-done((f32[32,16,256]{2,1,0:T(8,128)S(1)}, f32[32,16,256]{2,1,0:T(8,128)S(1)}, u32[]{:S(2)}, u32[]{:S(2)}) %collective-permute-start.5) | collective-permute-done | bytes 524320 | tf_op jit(solution)/shard_map/ppermute | solution.py:31
  79.2 14.0 %all_to_all.20 = f32[4,8,16,256]{3,2,1,0:T(8,128)S(1)} all-to-all(f32[4,8,16,256]{3,2,1,0:T(8,128)S(1)} %bitcast.19), channel_id=1, replica_groups={{0,16,32,48},{1,17,33,49},{2,18,34,50},{3,19,35,51},{4,20,36,52},{5,21,..., dimensions={0} | all-to-all | bytes 1048576 | tf_op jit(solution)/shard_map/all_to_all | solution.py:44
  93.2 0.7 reduce_sum.44
  93.9 10.8 %all-to-all-start.3 = ((f32[8,16,256]{2,1,0:T(8,128)}), f32[8,16,256]{2,1,0:T(8,128)S(1)}, u32[]{:S(2)}, u32[]{:S(2)}) async-start(f32[8,16,256]{2,1,0:T(8,128)} %reduce_sum.44), calls=%async_computation.3 | async-start | bytes 262144 | tf_op jit(solution)/shard_map/all_to_all | solution.py:44
  104.7 10.2 %all-to-all-done.3 = f32[8,16,256]{2,1,0:T(8,128)S(1)} async-done(((f32[8,16,256]{2,1,0:T(8,128)}), f32[8,16,256]{2,1,0:T(8,128)S(1)}, u32[]{:S(2)}, u32[]{:S(2)}) %all-to-all-start.3) | async-done | bytes 131104 | tf_op jit(solution)/shard_map/all_to_all | solution.py:44
  115.0 7.2 %collective-permute-start.6 = (f32[16,256]{1,0:T(8,128)S(1)}, f32[16,256]{1,0:T(8,128)S(1)}, u32[]{:S(2)}, u32[]{:S(2)}) collective-permute-start(f32[16,256]{1,0:T(8,128)S(1)} %pad_maximum_fusion.1), channel_id=1, source_target_pairs={{0,64},{1,65},{2,66},{3,67},{4,68},{5,69},{6,70},{7,71},{8,72},{9,... | collective-permute-start | bytes 49160 | tf_op jit(solution)/shard_map/ppermute | solution.py:31
  122.2 2.5 %collective-permute-start.7 = (f32[8,256]{1,0:T(8,128)S(1)}, f32[8,256]{1,0:T(8,128)S(1)}, u32[]{:S(2)}, u32[]{:S(2)}) collective-permute-start(f32[8,256]{1,0:T(8,128)S(1)} %get-tuple-element.37), channel_id=1, source_target_pairs={{0,128},{1,129},{2,130},{3,131},{4,132},{5,133},{6,134},{7,135},{8... | collective-permute-start | bytes 24584 | tf_op jit(solution)/shard_map/ppermute | solution.py:31
  124.8 4.9 %collective-permute-done.6 = f32[16,256]{1,0:T(8,128)S(1)} collective-permute-done((f32[16,256]{1,0:T(8,128)S(1)}, f32[16,256]{1,0:T(8,128)S(1)}, u32[]{:S(2)}, u32[]{:S(2)}) %collective-permute-start.6) | collective-permute-done | bytes 16416 | tf_op jit(solution)/shard_map/ppermute | solution.py:31
  129.7 0.6 copy.10
  (33 shorter events, 0.5 us)
Async XLA Ops:
  0.0 49.3 %copy-start.3 = (s32[768]{0:T(1024)S(1)}, s32[768]{0:T(1024)}, u32[]{:S(2)}) copy-start(s32[768]{0:T(1024)} %reach.1) | copy-start | bytes 9220
  0.0 49.3 %copy-start.4 = (f32[768]{0:T(1024)S(1)}, f32[768]{0:T(1024)}, u32[]{:S(2)}) copy-start(f32[768]{0:T(1024)} %param.8) | copy-start | bytes 9220
  0.0 57.7 %copy-start = (f32[2,768,256]{2,1,0:T(8,128)S(1)}, f32[2,768,256]{2,1,0:T(8,128)}, u32[]{:S(2)}) copy-start(f32[2,768,256]{2,1,0:T(8,128)} %ends.3) | copy-start | bytes 4718596
  0.0 57.7 %copy-start.1 = (f32[1,768,256]{2,1,0:T(8,128)S(1)}, f32[1,768,256]{2,1,0:T(8,128)}, u32[]{:S(2)}) copy-start(f32[1,768,256]{2,1,0:T(8,128)} %param.6) | copy-start | bytes 2359300
  0.0 57.7 %copy-start.2 = (f32[3,768]{1,0:T(4,128)S(1)}, f32[3,768]{1,0:T(4,128)}, u32[]{:S(2)}) copy-start(f32[3,768]{1,0:T(4,128)} %band.3) | copy-start | bytes 27652
  0.0 57.7 %collective-permute-start.3 = (f32[768,256]{1,0:T(8,128)}, f32[768,256]{1,0:T(8,128)S(1)}, u32[]{:S(2)}, u32[]{:S(2)}) collective-permute-start(f32[768,256]{1,0:T(8,128)} %bitcast.15), channel_id=1, source_target_pairs={{0,384},{1,385},{2,386},{3,387},{4,388},{5,389},{6,390},{7,391},{8... | collective-permute-start | bytes 2359304 | tf_op jit(solution)/shard_map/ppermute | solution.py:31
  7.1 21.6 %all-to-all-start = ((f32[8,1,256]{2,1,0:T(1,128)}), f32[8,1,256]{2,1,0:T(1,128)S(1)}, u32[]{:S(2)}, u32[]{:S(2)}) async-start(f32[8,1,256]{2,1,0:T(1,128)} %get-tuple-element.20), calls=%async_computation | async-start | bytes 16384 | tf_op jit(solution)/shard_map/all_to_all | solution.py:44
  19.7 9.0 %collective-permute-start = (f32[24,256]{1,0:T(8,128)}, f32[24,256]{1,0:T(8,128)S(1)}, u32[]{:S(2)}, u32[]{:S(2)}) collective-permute-start(f32[24,256]{1,0:T(8,128)} %get-tuple-element.21), channel_id=1, source_target_pairs={{0,1},{1,2},{2,3},{3,4},{4,5},{5,6},{6,7},{7,8},{8,9},{9,10},{10,1... | collective-permute-start | bytes 73736 | tf_op jit(solution)/shard_map/ppermute | solution.py:31
  28.7 43.8 %collective-permute-start.1 = (f32[392,256]{1,0:T(8,128)}, f32[392,256]{1,0:T(8,128)}, u32[]{:S(2)}, u32[]{:S(2)}) collective-permute-start(f32[392,256]{1,0:T(8,128)} %get-tuple-element.23), channel_id=1, source_target_pairs={{0,64},{1,65},{2,66},{3,67},{4,68},{5,69},{6,70},{7,71},{8,72},{9,... | collective-permute-start | bytes 1204232 | tf_op jit(solution)/shard_map/ppermute | solution.py:31
  36.1 9.6 %all-to-all-start.1 = ((f32[8,1,256]{2,1,0:T(1,128)}), f32[8,1,256]{2,1,0:T(1,128)S(1)}, u32[]{:S(2)}, u32[]{:S(2)}) async-start(f32[8,1,256]{2,1,0:T(1,128)} %broadcast_in_dim.45), calls=%async_computation.1 | async-start | bytes 16384 | tf_op jit(solution)/shard_map/all_to_all | solution.py:44
  45.8 12.0 %collective-permute-start.4 = (f32[16,256]{1,0:T(8,128)S(1)}, f32[16,256]{1,0:T(8,128)S(1)}, u32[]{:S(2)}, u32[]{:S(2)}) collective-permute-start(f32[16,256]{1,0:T(8,128)S(1)} %pad_maximum_fusion), channel_id=1, source_target_pairs={{0,384},{1,385},{2,386},{3,387},{4,388},{5,389},{6,390},{7,391},{8... | collective-permute-start | bytes 49160 | tf_op jit(solution)/shard_map/ppermute | solution.py:31
  49.4 23.2 %collective-permute-start.2 = (f32[16,256]{1,0:T(8,128)}, f32[16,256]{1,0:T(8,128)S(1)}, u32[]{:S(2)}, u32[]{:S(2)}) collective-permute-start(f32[16,256]{1,0:T(8,128)} %get-tuple-element.24), channel_id=1, source_target_pairs={{1,64},{2,65},{3,66},{4,67},{5,68},{6,69},{7,70},{8,71},{9,72},{10... | collective-permute-start | bytes 49160 | tf_op jit(solution)/shard_map/ppermute | solution.py:31
  75.3 3.8 %collective-permute-start.5 = (f32[32,16,256]{2,1,0:T(8,128)S(1)}, f32[32,16,256]{2,1,0:T(8,128)S(1)}, u32[]{:S(2)}, u32[]{:S(2)}) collective-permute-start(f32[32,16,256]{2,1,0:T(8,128)S(1)} %get-tuple-element.32), channel_id=1, source_target_pairs={{0,1},{1,0},{2,3},{3,2},{4,5},{5,4},{6,7},{7,6},{8,9},{9,8},{10,11... | collective-permute-start | bytes 1572872 | tf_op jit(solution)/shard_map/ppermute | solution.py:31
  93.9 21.0 %all-to-all-start.3 = ((f32[8,16,256]{2,1,0:T(8,128)}), f32[8,16,256]{2,1,0:T(8,128)S(1)}, u32[]{:S(2)}, u32[]{:S(2)}) async-start(f32[8,16,256]{2,1,0:T(8,128)} %reduce_sum.44), calls=%async_computation.3 | async-start | bytes 262144 | tf_op jit(solution)/shard_map/all_to_all | solution.py:44
  115.0 14.6 %collective-permute-start.6 = (f32[16,256]{1,0:T(8,128)S(1)}, f32[16,256]{1,0:T(8,128)S(1)}, u32[]{:S(2)}, u32[]{:S(2)}) collective-permute-start(f32[16,256]{1,0:T(8,128)S(1)} %pad_maximum_fusion.1), channel_id=1, source_target_pairs={{0,64},{1,65},{2,66},{3,67},{4,68},{5,69},{6,70},{7,71},{8,72},{9,... | collective-permute-start | bytes 49160 | tf_op jit(solution)/shard_map/ppermute | solution.py:31
  122.2 7.5 %collective-permute-start.7 = (f32[8,256]{1,0:T(8,128)S(1)}, f32[8,256]{1,0:T(8,128)S(1)}, u32[]{:S(2)}, u32[]{:S(2)}) collective-permute-start(f32[8,256]{1,0:T(8,128)S(1)} %get-tuple-element.37), channel_id=1, source_target_pairs={{0,128},{1,129},{2,130},{3,131},{4,132},{5,133},{6,134},{7,135},{8... | collective-permute-start | bytes 24584 | tf_op jit(solution)/shard_map/ppermute | solution.py:31

commit v5 on v4

--- a/solution.py
+++ b/solution.py
@@ -83,6 +83,18 @@
 
 def sign_of(values):
     return jnp.where(values > 0.0, 1.0, jnp.where(values < 0.0, -1.0, 0.0))
+
+
+def halves(a):
+    high = a.astype(jnp.bfloat16)
+    return high, (a - high.astype(jnp.float32)).astype(jnp.bfloat16)
+
+
+def product_of_halves(a, b):
+    def dot(x, y):
+        return lax.dot_general(x, y, (((0,), (0,)), ((), ())), preferred_element_type=jnp.float32)
+
+    return dot(a[0], b[0]) + (dot(a[0], b[1]) + dot(a[1], b[0]))
 
 
 def place():
@@ -221,9 +233,10 @@
         moved[pl.ds(at, size), :] = ends[h, pl.ds(pl.multiple_of(h * (half - edge), edge), size), :]
 
     scale = 1.0 / (2.0 * radial_step)
-    cross = product(seen[...], slope_applied[...])
-    first = product(own_applied[...], seen[...] * scale)
-    second = product(near_applied[...], moved[...] * scale)
+    view = halves(seen[...])
+    cross = product_of_halves(view, halves(slope_applied[...]))
+    first = product_of_halves(halves(own_applied[...]), view) * scale
+    second = product_of_halves(halves(near_applied[...]), halves(moved[...])) * scale
     low = core == 0
     for index, part in enumerate((cross, curve[...], first, second)):
         part = part.reshape(32, 2 * 4, part.shape[1])

time: 131 us -> 130 us (level)
  no operation moved by 1% of the time
where the time goes in v5:
time: 130 us
  starting transfers between devices  64.9 us (50%)
  waiting for transfers between devices  39.9 us (31%)
  blocking collectives  14 us (11%)
  Pallas kernels  8.15 us (6%)
  local copies, waits for them, and re-layouts  1.33 us (1%)
    ppermute x8, starting transfers between devices, move(): return lax.ppermute(array, both, hops(target))  37.2 us
    all_to_all x3, starting transfers between devices, spread(): return lax.all_to_all(array, 'basis', 0, 0, axis_index_groups=groups)  27.7 us
    all_to_all x3, waiting for transfers between devices, spread(): return lax.all_to_all(array, 'basis', 0, 0, axis_index_groups=groups)  22.6 us
    ppermute x8, waiting for transfers between devices, move(): return lax.ppermute(array, both, hops(target))  17.3 us
    all_to_all x1, blocking collectives, spread(): return lax.all_to_all(array, 'basis', 0, 0, axis_index_groups=groups)  14 us
    pallas_call x2, Pallas kernels, kernel(): pl.pallas_call(body, out_shape=[jax.ShapeDtypeStruct(shape, jnp.float32)...  6.14 us
  transfers between devices with their start and end apart: 11, of which 6 were waited for; matrix products, arithmetic and copies ran while one was open for 1% of the time, Pallas kernels for 5%

profile of v5, /device:TPU:32, one launch (start us, length us, event | category | flops | bytes accessed | tf_op | source)
XLA Modules:
  0.0 129.5 jit_solution(15404695104899342426)
XLA Ops:
  0.0 5.1 %collective-permute-start.3 = (f32[768,256]{1,0:T(8,128)}, f32[768,256]{1,0:T(8,128)S(1)}, u32[]{:S(2)}, u32[]{:S(2)}) collective-permute-start(f32[768,256]{1,0:T(8,128)} %bitcast.15), channel_id=1, source_target_pairs={{0,384},{1,385},{2,386},{3,387},{4,388},{5,389},{6,390},{7,391},{8... | collective-permute-start | bytes 2359304 | tf_op jit(solution)/shard_map/ppermute | solution.py:31
  5.1 2.0 %shard_map.64 = (f32[392,256]{1,0:T(8,128)}, f32[24,256]{1,0:T(8,128)}, f32[16,256]{1,0:T(8,128)}, f32[8,1,256]{2,1,0:T(1,128)}) custom-call(f32[768,256]{1,0:T(8,128)} %bitcast.16, f32[2,768,256]{2,1,0:T(8,128)} %ends.3, f32[2,768,256]{2,1,0:T(8,128)} %ends.3, f32[3,768]{1,0:T(4,128)} %band.3, s32[768]{0:T(1024)} %reach.1, s32[1,256]{1,0:T(1,128)} %rows_of.1), custom_call_target="tpu_custom_call" | custom-call | flops 1000000 | bytes 2097152 | tf_op jit(solution)/shard_map/pallas_call | solution.py:269
  7.1 12.6 %all-to-all-start = ((f32[8,1,256]{2,1,0:T(1,128)}), f32[8,1,256]{2,1,0:T(1,128)S(1)}, u32[]{:S(2)}, u32[]{:S(2)}) async-start(f32[8,1,256]{2,1,0:T(1,128)} %get-tuple-element.20), calls=%async_computation | async-start | bytes 16384 | tf_op jit(solution)/shard_map/all_to_all | solution.py:44
  19.7 1.9 %collective-permute-start = (f32[24,256]{1,0:T(8,128)}, f32[24,256]{1,0:T(8,128)S(1)}, u32[]{:S(2)}, u32[]{:S(2)}) collective-permute-start(f32[24,256]{1,0:T(8,128)} %get-tuple-element.21), channel_id=1, source_target_pairs={{0,1},{1,2},{2,3},{3,4},{4,5},{5,6},{6,7},{7,8},{8,9},{9,10},{10,1... | collective-permute-start | bytes 73736 | tf_op jit(solution)/shard_map/ppermute | solution.py:31
  21.6 7.0 %all-to-all-done = f32[8,1,256]{2,1,0:T(1,128)S(1)} async-done(((f32[8,1,256]{2,1,0:T(1,128)}), f32[8,1,256]{2,1,0:T(1,128)S(1)}, u32[]{:S(2)}, u32[]{:S(2)}) %all-to-all-start) | async-done | bytes 8224 | tf_op jit(solution)/shard_map/all_to_all | solution.py:44
  28.7 6.8 %collective-permute-start.1 = (f32[392,256]{1,0:T(8,128)}, f32[392,256]{1,0:T(8,128)}, u32[]{:S(2)}, u32[]{:S(2)}) collective-permute-start(f32[392,256]{1,0:T(8,128)} %get-tuple-element.23), channel_id=1, source_target_pairs={{0,64},{1,65},{2,66},{3,67},{4,68},{5,69},{6,70},{7,71},{8,72},{9,... | collective-permute-start | bytes 1204232 | tf_op jit(solution)/shard_map/ppermute | solution.py:31
  35.5 0.6 broadcast_in_dim.45
  36.1 4.3 %all-to-all-start.1 = ((f32[8,1,256]{2,1,0:T(1,128)}), f32[8,1,256]{2,1,0:T(1,128)S(1)}, u32[]{:S(2)}, u32[]{:S(2)}) async-start(f32[8,1,256]{2,1,0:T(1,128)} %broadcast_in_dim.45), calls=%async_computation.1 | async-start | bytes 16384 | tf_op jit(solution)/shard_map/all_to_all | solution.py:44
  40.4 5.3 %all-to-all-done.1 = f32[8,1,256]{2,1,0:T(1,128)S(1)} async-done(((f32[8,1,256]{2,1,0:T(1,128)}), f32[8,1,256]{2,1,0:T(1,128)S(1)}, u32[]{:S(2)}, u32[]{:S(2)}) %all-to-all-start.1) | async-done | bytes 8224 | tf_op jit(solution)/shard_map/all_to_all | solution.py:44
  45.8 3.6 %collective-permute-start.4 = (f32[16,256]{1,0:T(8,128)S(1)}, f32[16,256]{1,0:T(8,128)S(1)}, u32[]{:S(2)}, u32[]{:S(2)}) collective-permute-start(f32[16,256]{1,0:T(8,128)S(1)} %pad_maximum_fusion), channel_id=1, source_target_pairs={{0,384},{1,385},{2,386},{3,387},{4,388},{5,389},{6,390},{7,391},{8... | collective-permute-start | bytes 49160 | tf_op jit(solution)/shard_map/ppermute | solution.py:31
  49.4 8.3 %collective-permute-start.2 = (f32[16,256]{1,0:T(8,128)}, f32[16,256]{1,0:T(8,128)S(1)}, u32[]{:S(2)}, u32[]{:S(2)}) collective-permute-start(f32[16,256]{1,0:T(8,128)} %get-tuple-element.24), channel_id=1, source_target_pairs={{1,64},{2,65},{3,66},{4,67},{5,68},{6,69},{7,70},{8,71},{9,72},{10... | collective-permute-start | bytes 49160 | tf_op jit(solution)/shard_map/ppermute | solution.py:31
  57.8 4.2 %shard_map.65 = (f32[400,256]{1,0:T(8,128)S(1)}, f32[400,256]{1,0:T(8,128)S(1)}, f32[400,256]{1,0:T(8,128)S(1)}, f32[256,256]{1,0:T(8,128)S(1)}) custom-call(f32[768,256]{1,0:T(8,128)S(1)} %bitcast.17, f32[768,256]{1,0:T(8,128)S(1)} %collective-permute-done.3.near, f32[2,768,256]{2,1,0:T(8,128)S(1)} %copy-done, f32[24,256]{1,0:T(8,128)S(1)} %collective-permute-done.own_rim, ...), custom_call_target="tpu_custom_call" | custom-call | flops 1000000000 | bytes 4194304 | tf_op jit(solution)/shard_map/pallas_call | solution.py:249
  62.0 10.6 %collective-permute-done.2.visitor_rim = f32[16,256]{1,0:T(8,128)S(1)} collective-permute-done((f32[16,256]{1,0:T(8,128)}, f32[16,256]{1,0:T(8,128)S(1)}, u32[]{:S(2)}, u32[]{:S(2)}) %collective-permute-start.2) | collective-permute-done | bytes 16416 | tf_op jit(solution)/shard_map/ppermute | solution.py:31
  72.5 2.0 %shard_map.66 = (f32[32,16,256]{2,1,0:T(8,128)S(1)}, f32[32,16,256]{2,1,0:T(8,128)S(1)}) custom-call(f32[392,256]{1,0:T(8,128)} %collective-permute-done.1.visitor, f32[16,256]{1,0:T(8,128)S(1)} %collective-permute-done.2.visitor_rim, f32[2,768,256]{2,1,0:T(8,128)S(1)} %copy-done, f32[400,256]{1,0:T(8,128)S(1)} %get-tuple-element.27.slope_applied, ...), custom_call_target="tpu_custom_call" | custom-call | flops 1000000000 | bytes 4194304 | tf_op jit(solution)/shard_map/pallas_call | solution.py:249
  74.5 1.9 %collective-permute-start.5 = (f32[32,16,256]{2,1,0:T(8,128)S(1)}, f32[32,16,256]{2,1,0:T(8,128)S(1)}, u32[]{:S(2)}, u32[]{:S(2)}) collective-permute-start(f32[32,16,256]{2,1,0:T(8,128)S(1)} %get-tuple-element.32), channel_id=1, source_target_pairs={{0,1},{1,0},{2,3},{3,2},{4,5},{5,4},{6,7},{7,6},{8,9},{9,8},{10,11... | collective-permute-start | bytes 1572872 | tf_op jit(solution)/shard_map/ppermute | solution.py:31
  76.5 1.9 %collective-permute-done.5 = f32[32,16,256]{2,1,0:T(8,128)S(1)} collective-permute-done((f32[32,16,256]{2,1,0:T(8,128)S(1)}, f32[32,16,256]{2,1,0:T(8,128)S(1)}, u32[]{:S(2)}, u32[]{:S(2)}) %collective-permute-start.5) | collective-permute-done | bytes 524320 | tf_op jit(solution)/shard_map/ppermute | solution.py:31
  78.4 14.0 %all_to_all.20 = f32[4,8,16,256]{3,2,1,0:T(8,128)S(1)} all-to-all(f32[4,8,16,256]{3,2,1,0:T(8,128)S(1)} %bitcast.19), channel_id=1, replica_groups={{0,16,32,48},{1,17,33,49},{2,18,34,50},{3,19,35,51},{4,20,36,52},{5,21,..., dimensions={0} | all-to-all | bytes 1048576 | tf_op jit(solution)/shard_map/all_to_all | solution.py:44
  92.4 0.7 reduce_sum.44
  93.1 10.8 %all-to-all-start.3 = ((f32[8,16,256]{2,1,0:T(8,128)}), f32[8,16,256]{2,1,0:T(8,128)S(1)}, u32[]{:S(2)}, u32[]{:S(2)}) async-start(f32[8,16,256]{2,1,0:T(8,128)} %reduce_sum.44), calls=%async_computation.3 | async-start | bytes 262144 | tf_op jit(solution)/shard_map/all_to_all | solution.py:44
  103.9 10.2 %all-to-all-done.3 = f32[8,16,256]{2,1,0:T(8,128)S(1)} async-done(((f32[8,16,256]{2,1,0:T(8,128)}), f32[8,16,256]{2,1,0:T(8,128)S(1)}, u32[]{:S(2)}, u32[]{:S(2)}) %all-to-all-start.3) | async-done | bytes 131104 | tf_op jit(solution)/shard_map/all_to_all | solution.py:44
  114.2 7.2 %collective-permute-start.6 = (f32[16,256]{1,0:T(8,128)S(1)}, f32[16,256]{1,0:T(8,128)S(1)}, u32[]{:S(2)}, u32[]{:S(2)}) collective-permute-start(f32[16,256]{1,0:T(8,128)S(1)} %pad_maximum_fusion.1), channel_id=1, source_target_pairs={{0,64},{1,65},{2,66},{3,67},{4,68},{5,69},{6,70},{7,71},{8,72},{9,... | collective-permute-start | bytes 49160 | tf_op jit(solution)/shard_map/ppermute | solution.py:31
  121.4 2.5 %collective-permute-start.7 = (f32[8,256]{1,0:T(8,128)S(1)}, f32[8,256]{1,0:T(8,128)S(1)}, u32[]{:S(2)}, u32[]{:S(2)}) collective-permute-start(f32[8,256]{1,0:T(8,128)S(1)} %get-tuple-element.37), channel_id=1, source_target_pairs={{0,128},{1,129},{2,130},{3,131},{4,132},{5,133},{6,134},{7,135},{8... | collective-permute-start | bytes 24584 | tf_op jit(solution)/shard_map/ppermute | solution.py:31
  124.0 4.9 %collective-permute-done.6 = f32[16,256]{1,0:T(8,128)S(1)} collective-permute-done((f32[16,256]{1,0:T(8,128)S(1)}, f32[16,256]{1,0:T(8,128)S(1)}, u32[]{:S(2)}, u32[]{:S(2)}) %collective-permute-start.6) | collective-permute-done | bytes 16416 | tf_op jit(solution)/shard_map/ppermute | solution.py:31
  128.9 0.6 copy.10
  (33 shorter events, 0.5 us)
Async XLA Ops:
  0.0 49.3 %copy-start.3 = (s32[768]{0:T(1024)S(1)}, s32[768]{0:T(1024)}, u32[]{:S(2)}) copy-start(s32[768]{0:T(1024)} %reach.1) | copy-start | bytes 9220
  0.0 49.3 %copy-start.4 = (f32[768]{0:T(1024)S(1)}, f32[768]{0:T(1024)}, u32[]{:S(2)}) copy-start(f32[768]{0:T(1024)} %param.8) | copy-start | bytes 9220
  0.0 57.7 %copy-start = (f32[2,768,256]{2,1,0:T(8,128)S(1)}, f32[2,768,256]{2,1,0:T(8,128)}, u32[]{:S(2)}) copy-start(f32[2,768,256]{2,1,0:T(8,128)} %ends.3) | copy-start | bytes 4718596
  0.0 57.7 %copy-start.1 = (f32[1,768,256]{2,1,0:T(8,128)S(1)}, f32[1,768,256]{2,1,0:T(8,128)}, u32[]{:S(2)}) copy-start(f32[1,768,256]{2,1,0:T(8,128)} %param.6) | copy-start | bytes 2359300
  0.0 57.7 %copy-start.2 = (f32[3,768]{1,0:T(4,128)S(1)}, f32[3,768]{1,0:T(4,128)}, u32[]{:S(2)}) copy-start(f32[3,768]{1,0:T(4,128)} %band.3) | copy-start | bytes 27652
  0.0 57.7 %collective-permute-start.3 = (f32[768,256]{1,0:T(8,128)}, f32[768,256]{1,0:T(8,128)S(1)}, u32[]{:S(2)}, u32[]{:S(2)}) collective-permute-start(f32[768,256]{1,0:T(8,128)} %bitcast.15), channel_id=1, source_target_pairs={{0,384},{1,385},{2,386},{3,387},{4,388},{5,389},{6,390},{7,391},{8... | collective-permute-start | bytes 2359304 | tf_op jit(solution)/shard_map/ppermute | solution.py:31
  7.1 21.6 %all-to-all-start = ((f32[8,1,256]{2,1,0:T(1,128)}), f32[8,1,256]{2,1,0:T(1,128)S(1)}, u32[]{:S(2)}, u32[]{:S(2)}) async-start(f32[8,1,256]{2,1,0:T(1,128)} %get-tuple-element.20), calls=%async_computation | async-start | bytes 16384 | tf_op jit(solution)/shard_map/all_to_all | solution.py:44
  19.7 9.0 %collective-permute-start = (f32[24,256]{1,0:T(8,128)}, f32[24,256]{1,0:T(8,128)S(1)}, u32[]{:S(2)}, u32[]{:S(2)}) collective-permute-start(f32[24,256]{1,0:T(8,128)} %get-tuple-element.21), channel_id=1, source_target_pairs={{0,1},{1,2},{2,3},{3,4},{4,5},{5,6},{6,7},{7,8},{8,9},{9,10},{10,1... | collective-permute-start | bytes 73736 | tf_op jit(solution)/shard_map/ppermute | solution.py:31
  28.7 43.8 %collective-permute-start.1 = (f32[392,256]{1,0:T(8,128)}, f32[392,256]{1,0:T(8,128)}, u32[]{:S(2)}, u32[]{:S(2)}) collective-permute-start(f32[392,256]{1,0:T(8,128)} %get-tuple-element.23), channel_id=1, source_target_pairs={{0,64},{1,65},{2,66},{3,67},{4,68},{5,69},{6,70},{7,71},{8,72},{9,... | collective-permute-start | bytes 1204232 | tf_op jit(solution)/shard_map/ppermute | solution.py:31
  36.1 9.6 %all-to-all-start.1 = ((f32[8,1,256]{2,1,0:T(1,128)}), f32[8,1,256]{2,1,0:T(1,128)S(1)}, u32[]{:S(2)}, u32[]{:S(2)}) async-start(f32[8,1,256]{2,1,0:T(1,128)} %broadcast_in_dim.45), calls=%async_computation.1 | async-start | bytes 16384 | tf_op jit(solution)/shard_map/all_to_all | solution.py:44
  45.8 12.0 %collective-permute-start.4 = (f32[16,256]{1,0:T(8,128)S(1)}, f32[16,256]{1,0:T(8,128)S(1)}, u32[]{:S(2)}, u32[]{:S(2)}) collective-permute-start(f32[16,256]{1,0:T(8,128)S(1)} %pad_maximum_fusion), channel_id=1, source_target_pairs={{0,384},{1,385},{2,386},{3,387},{4,388},{5,389},{6,390},{7,391},{8... | collective-permute-start | bytes 49160 | tf_op jit(solution)/shard_map/ppermute | solution.py:31
  49.4 23.2 %collective-permute-start.2 = (f32[16,256]{1,0:T(8,128)}, f32[16,256]{1,0:T(8,128)S(1)}, u32[]{:S(2)}, u32[]{:S(2)}) collective-permute-start(f32[16,256]{1,0:T(8,128)} %get-tuple-element.24), channel_id=1, source_target_pairs={{1,64},{2,65},{3,66},{4,67},{5,68},{6,69},{7,70},{8,71},{9,72},{10... | collective-permute-start | bytes 49160 | tf_op jit(solution)/shard_map/ppermute | solution.py:31
  74.5 3.8 %collective-permute-start.5 = (f32[32,16,256]{2,1,0:T(8,128)S(1)}, f32[32,16,256]{2,1,0:T(8,128)S(1)}, u32[]{:S(2)}, u32[]{:S(2)}) collective-permute-start(f32[32,16,256]{2,1,0:T(8,128)S(1)} %get-tuple-element.32), channel_id=1, source_target_pairs={{0,1},{1,0},{2,3},{3,2},{4,5},{5,4},{6,7},{7,6},{8,9},{9,8},{10,11... | collective-permute-start | bytes 1572872 | tf_op jit(solution)/shard_map/ppermute | solution.py:31
  93.1 21.0 %all-to-all-start.3 = ((f32[8,16,256]{2,1,0:T(8,128)}), f32[8,16,256]{2,1,0:T(8,128)S(1)}, u32[]{:S(2)}, u32[]{:S(2)}) async-start(f32[8,16,256]{2,1,0:T(8,128)} %reduce_sum.44), calls=%async_computation.3 | async-start | bytes 262144 | tf_op jit(solution)/shard_map/all_to_all | solution.py:44
  114.2 14.6 %collective-permute-start.6 = (f32[16,256]{1,0:T(8,128)S(1)}, f32[16,256]{1,0:T(8,128)S(1)}, u32[]{:S(2)}, u32[]{:S(2)}) collective-permute-start(f32[16,256]{1,0:T(8,128)S(1)} %pad_maximum_fusion.1), channel_id=1, source_target_pairs={{0,64},{1,65},{2,66},{3,67},{4,68},{5,69},{6,70},{7,71},{8,72},{9,... | collective-permute-start | bytes 49160 | tf_op jit(solution)/shard_map/ppermute | solution.py:31
  121.4 7.5 %collective-permute-start.7 = (f32[8,256]{1,0:T(8,128)S(1)}, f32[8,256]{1,0:T(8,128)S(1)}, u32[]{:S(2)}, u32[]{:S(2)}) collective-permute-start(f32[8,256]{1,0:T(8,128)S(1)} %get-tuple-element.37), channel_id=1, source_target_pairs={{0,128},{1,129},{2,130},{3,131},{4,132},{5,133},{6,134},{7,135},{8... | collective-permute-start | bytes 24584 | tf_op jit(solution)/shard_map/ppermute | solution.py:31
